TPU v7x, 128 devices: a whole 4x4x4 slice. The times are simulated.
128 devices in a mesh: clip: 4 (over y_hi, core), tile: 32 (over y_lo, x, z).
Axes of the slice: x: 4, y: 4 (y_hi: 2, y_lo: 2; y = y_hi * 2 + y_lo), z: 4, core: 2. Of those that a mesh axis runs over, the one named last changes fastest.
Arguments:
- features: bfloat16 [8, 16, 64, 12, 384], P('clip', None, 'tile'), may hold values from -6 to 6
- pixel_grad: bfloat16 [8, 16, 64, 12, 384], P('clip', None, 'tile'), may hold values from -6 to 6
- frame_list: int32 [8, 16], P('clip'), may hold values from -1 to 15, as said below
- conv_weight: bfloat16 [3, 3, 3, 384, 384], replicated, may hold values from -0.0625 to 0.0625
- in_weight: bfloat16 [3, 3, 3, 16, 384], replicated, may hold values from -0.3125 to 0.3125
- last_hidden: bfloat16 [24576, 5120], P(('clip', 'tile')), may hold values from -6 to 6
- modulation: float32 [8, 2, 5120], P('clip'), may hold values from -3 to 3
- head_weight: bfloat16 [5120, 64], replicated, may hold values from -0.75 to 0.75
Outputs:
- hidden_grad: bfloat16 [24576, 5120], P(('clip', 'tile'))
- head_weight_grad: float32 [5120, 64], replicated
- modulation_grad: float32 [8, 2, 5120], P('clip')
- conv_weight_grad: float32 [3, 3, 3, 384, 384], P(None, None, None, 'tile')
Inputs may be any that keep to these rules, and one draw needn't show every extreme that they name: `frame_list`: each clip's list holds between 2 and 16 distinct frame numbers first, then -1; some clip lists every frame.
All inputs are finite; a program needn't handle non-finite values.
Results may differ from a plain program's by a relative error of at most 0.006.
Values may be sent and summed in bfloat16 or wider, within the bound.
No kernel may reach another device: no remote copies, remote signals or barrier semaphores. Data moves between devices by JAX's collectives and lax.ppermute only.
A program may use at most 192 MiB of HBM per device.

v0:
```python
import functools

import jax
import jax.numpy as jnp
from jax import lax
from jax.experimental import pallas as pl
from jax.experimental.pallas import tpu as pltpu
from jax.sharding import PartitionSpec as P

F32 = jnp.float32
BF16 = jnp.bfloat16
BOTH = ("clip", "tile")
FRAMES = 16
SPAN = 32
COLS = 12
CH = 384
WIDTH = 5120
HALF = 2560
STEP = 1280
TAPS = 14
LARGE = 56 * 1024 * 1024
IN_VMEM = pl.BlockSpec(memory_space=pltpu.VMEM)


def place(clip, tile):
    return (clip // 2) * 2 + tile // 16, (tile // 4) % 4, tile % 4, clip % 2


def number(y, x, z, core):
    return ((y // 2) * 2 + core) * 32 + (y % 2) * 16 + x * 4 + z


def pairs(shift_of):
    out = []
    for source in range(128):
        where = place(source // 32, source % 32)
        out.append((source, number(*shift_of(*where))))
    return out


def along(core_axis, steps):
    def shift(y, x, z, core):
        if core == core_axis:
            return y, x, (z + steps) % 4, core
        return y, (x + steps) % 4, z, core

    return pairs(shift)


def along_y(steps):
    return pairs(lambda y, x, z, core: ((y + steps) % 4, x, z, core))


SAME_CORE = [[c * 32 + t for c in (core, core + 2) for t in range(32)] for core in (0, 1)]
OTHER_CORE = pairs(lambda y, x, z, core: (y, x, z, 1 - core))


def shift_frames(tile, steps):
    if steps == 0:
        return tile
    count = tile.shape[0]
    moved = pltpu.roll(tile, count - steps, 0)
    frame = lax.broadcasted_iota(jnp.int32, tile.shape, 0) & (FRAMES - 1)
    return jnp.where(frame < FRAMES - steps, moved, 0.0)


def fill_row(padded, source, base, keep=None):
    blank = jnp.zeros((SPAN, CH), BF16)
    padded[0, pl.ds(base, SPAN)] = blank
    padded[COLS + 1, pl.ds(base, SPAN)] = blank
    rows = source[...]
    padded[pl.ds(1, COLS), pl.ds(base, SPAN)] = rows if keep is None else rows * keep[...]


def lanes_dot(left, right):
    return lax.dot_general(left, right, (((1,), (1,)), ((), ())), preferred_element_type=F32)


def column_windows(rows):
    return jnp.concatenate(
        [rows[:, 2 - col_tap : 2 - col_tap + COLS].reshape(-1, CH) for col_tap in range(3)], axis=1
    )


def tap_weights(weight):
    return jnp.concatenate(
        [
            jnp.concatenate([weight[time_tap, 0, col_tap] for col_tap in range(3)], axis=1)
            for time_tap in range(3)
        ],
        axis=0,
    )


def grad_kernel(
    own, low, high, keep, feats, weight, in_weight, out, padded, total, grads, spread
):
    step = pl.program_id(0)

    @pl.when(step == 0)
    def _():
        for row, source in enumerate((low, own.at[0], own.at[1], high)):
            fill_row(padded.at[row], source, 0, None if row in (1, 2) else keep)
        total[...] = lanes_dot(column_windows(padded.at[1:3]), tap_weights(weight))
        blank = jnp.zeros((16, CH), BF16)
        for time_tap in range(3):
            for rowout in range(4):
                for parity in range(2):
                    at = ((time_tap * 4 + rowout) * 2 + parity) * 16
                    for near in range(4):
                        for side in range(2):
                            row_tap = rowout - side
                            col_tap = parity + 2 - near
                            inside = 0 <= row_tap <= 2 and 0 <= col_tap <= 2
                            value = in_weight[time_tap, row_tap, col_tap] if inside else blank
                            spread[at : at + 16, pl.ds((near * 2 + side) * CH, CH)] = value

    @pl.when(step == 1)
    def _():
        total[...] += lanes_dot(column_windows(padded.at[2:4]), tap_weights(weight))

    def finish(side, source):
        blank = jnp.zeros((SPAN, CH), BF16)
        grads[side, 0, 0] = blank
        grads[side, 6, 1] = blank
        for col in range(COLS):
            values = feats[side, col].astype(F32)
            sig = jax.nn.sigmoid(values)
            slope = sig * (1.0 + values * (1.0 - sig))
            tile = source[col * SPAN : (col + 1) * SPAN]
            summed = (
                tile[:, 0:CH]
                + shift_frames(tile[:, CH : 2 * CH], 1)
                + shift_frames(tile[:, 2 * CH : 3 * CH], 2)
            )
            grads[side, (col + 1) // 2, (col + 1) % 2] = (summed * slope).astype(BF16)

    @pl.when(step == 2)
    def _():
        total[...] += lanes_dot(column_windows(padded.at[0:2]), tap_weights(weight))
        for side in range(2):
            finish(side, total.at[side * 384 : (side + 1) * 384])
        left = jnp.concatenate(
            [
                grads[side, pl.ds(near // 2, 6), near % 2].reshape(-1, CH)
                for near in range(4)
                for side in range(2)
            ],
            axis=1,
        )
        latent = lanes_dot(left, spread[...])
        for pair in range(6):
            block = latent[pair * SPAN : (pair + 1) * SPAN]
            out[:, pair, :] = (
                block[:, 0:128]
                + shift_frames(block[:, 128:256], 1)
                + shift_frames(block[:, 256:384], 2)
            )
        out[:, 6:8, :] = jnp.zeros((SPAN, 2, 128), F32)


def whole(*shape):
    return pl.BlockSpec(shape, lambda i: (0,) * len(shape))


def input_grad(own, low, high, keep, feats, conv_weight, in_weight):
    return pl.pallas_call(
        grad_kernel,
        grid=(3,),
        in_specs=[
            whole(2, COLS, SPAN, CH),
            whole(COLS, SPAN, CH),
            whole(COLS, SPAN, CH),
            whole(SPAN, CH),
            whole(2, COLS, SPAN, CH),
            pl.BlockSpec((3, 1, 3, CH, CH), lambda i: (0, jnp.where(i == 2, 2, 1 - i), 0, 0, 0)),
            whole(3, 3, 3, 16, CH),
        ],
        out_specs=whole(SPAN, 8, 128),
        out_shape=jax.ShapeDtypeStruct((SPAN, 8, 128), F32),
        scratch_shapes=[
            pltpu.VMEM((4, COLS + 2, SPAN, CH), BF16),
            pltpu.VMEM((2 * COLS * SPAN, 3 * CH), F32),
            pltpu.VMEM((2, 7, 2, SPAN, CH), BF16),
            pltpu.VMEM((384, 8 * CH), BF16),
        ],
        compiler_params=pltpu.CompilerParams(vmem_limit_bytes=LARGE),
        cost_estimate=pl.CostEstimate(
            flops=2 * 768 * 27 * CH * CH, bytes_accessed=12_000_000, transcendentals=768 * CH
        ),
        name="input_grad",
    )(own, low, high, keep, feats, conv_weight, in_weight)


def weight_kernel(
    core, own, low, high, keep, acts, own2, low2, high2, keep2, acts2, order,
    out0, out1, out2, out3, padded, active, turned,
):
    step = pl.program_id(0)

    @pl.when(step == 0)
    def _():
        for base, rows, kept in ((0, (low, own.at[0], own.at[1], high), keep),
                                 (SPAN, (low2, own2.at[0], own2.at[1], high2), keep2)):
            for row, source in enumerate(rows):
                fill_row(padded.at[row], source, base, None if row in (1, 2) else kept)
        for base, source in ((0, acts), (SPAN, acts2)):
            active[:, :, pl.ds(base, SPAN)] = source[...]
        frame = lax.broadcasted_iota(jnp.int32, (CH, 128), 1) & (FRAMES - 1)
        across = lanes_dot(order[...], active[...].reshape(-1, CH))
        for at in range(0, 2 * COLS * 2 * SPAN, 128):
            values = across[:, at : at + 128]
            one = jnp.where(frame >= 1, pltpu.roll(values, 1, 1), 0.0)
            two = jnp.where(frame >= 2, pltpu.roll(values, 2, 1), 0.0)
            turned[0, :, at : at + 128] = jnp.where(core[0] == 0, values, two).astype(BF16)
            turned[1, :, at : at + 128] = one.astype(BF16)

    def window(place_at):
        tap = jnp.where(place_at < 9, place_at, place_at - 9 + 4 * core[0])
        row_tap = lax.div(tap, 3)
        col_tap = tap - 3 * row_tap
        return padded[pl.ds(2 - row_tap, 2), pl.ds(2 - col_tap, COLS)].reshape(-1, CH)

    def write(which, product):
        for part, out in enumerate((out0, out1, out2, out3)):
            out[which] = product[part * 96 : (part + 1) * 96].astype(BF16)

    @pl.when(step != 4)
    def _():
        right = jnp.concatenate([window(2 * step), window(2 * step + 1)], axis=1)
        slot = jnp.where(step < 4, 0, 1)
        product = jnp.dot(turned[slot], right, preferred_element_type=F32)
        write(0, product[:, 0:CH])
        write(1, product[:, CH : 2 * CH])

    @pl.when(step == 4)
    def _():
        for slot in range(2):
            write(slot, jnp.dot(turned[slot], window(8 + slot), preferred_element_type=F32))


def weight_grad(core, own, low, high, keep, acts, own2, low2, high2, keep2, acts2, order):
    rows = [whole(2, COLS, SPAN, CH), whole(COLS, SPAN, CH), whole(COLS, SPAN, CH),
            whole(SPAN, CH), whole(2, COLS, SPAN, CH)]
    return pl.pallas_call(
        weight_kernel,
        grid=(TAPS // 2,),
        in_specs=[pl.BlockSpec(memory_space=pltpu.SMEM), *rows, *rows, whole(CH, CH)],
        out_specs=[pl.BlockSpec((2, 96, CH), lambda i: (i, 0, 0))] * 4,
        out_shape=[jax.ShapeDtypeStruct((TAPS, 96, CH), BF16)] * 4,
        scratch_shapes=[
            pltpu.VMEM((4, COLS + 2, 2 * SPAN, CH), BF16),
            pltpu.VMEM((2, COLS, 2 * SPAN, CH), BF16),
            pltpu.VMEM((2, CH, 2 * COLS * 2 * SPAN), BF16),
        ],
        compiler_params=pltpu.CompilerParams(vmem_limit_bytes=LARGE),
        cost_estimate=pl.CostEstimate(
            flops=2 * 1536 * TAPS * CH * CH, bytes_accessed=12_000_000, transcendentals=1536 * CH
        ),
        name="weight_grad",
    )(core, own, low, high, keep, acts, own2, low2, high2, keep2, acts2, order)


def stats_kernel(states, stat):
    blocks = [slice(at, at + 128) for at in range(0, WIDTH, 128)]
    summed = jnp.zeros((32, 128), F32)
    for block in blocks:
        summed = summed + states[:, block].astype(F32)
    average = jnp.sum(summed, axis=-1, keepdims=True) * (1.0 / WIDTH)
    spread = jnp.broadcast_to(average, (32, 128))
    summed = jnp.zeros((32, 128), F32)
    for block in blocks:
        centered = states[:, block].astype(F32) - spread
        summed = summed + centered * centered
    variance = jnp.sum(summed, axis=-1, keepdims=True) * (1.0 / WIDTH)
    inv_std = jnp.broadcast_to(lax.rsqrt(variance + 1e-06), (32, 128))
    stat[:, 0:128] = spread
    stat[:, 128:256] = inv_std


def stats(states):
    tokens = states.shape[0]
    return pl.pallas_call(
        stats_kernel,
        grid=(tokens // 32,),
        in_specs=[pl.BlockSpec((32, WIDTH), lambda i: (i, 0))],
        out_specs=pl.BlockSpec((32, 256), lambda i: (i, 0)),
        out_shape=jax.ShapeDtypeStruct((tokens, 256), F32),
        compiler_params=pltpu.CompilerParams(vmem_limit_bytes=8 * 1024 * 1024),
        cost_estimate=pl.CostEstimate(flops=1, bytes_accessed=1, transcendentals=0),
        name="token_stats",
    )(states)


def head_kernel(
    core, sent, states, head_weight, mods, stat,
    load, give, terms, patch, patch_t, total, gains, whole, piece, sums, dots,
):
    step = pl.program_id(0)
    tokens = patch.shape[0]

    @pl.when(step == 0)
    def _():
        below = lax.broadcasted_iota(jnp.int32, (SPAN, 128), 0)
        lane = lax.broadcasted_iota(jnp.int32, (SPAN, 128), 1)
        parts = []
        for pair in range(6):
            here = sent[:, pair, :]
            swapped = pltpu.roll(here, 64, 1)
            before = jnp.where(below > 0, pltpu.roll(swapped, 1, 0), 0.0)
            after = jnp.where(below < SPAN - 1, pltpu.roll(swapped, SPAN - 1, 0), 0.0)
            summed = here + jnp.where(lane < 64, before, after)
            inside = (lane >= 32) & (lane < 96)
            parts.append(jnp.where(inside, summed, 0.0).astype(BF16))
        stacked = jnp.concatenate(parts, axis=0)
        token = lax.broadcasted_iota(jnp.int32, (tokens, tokens), 0)
        source = lax.broadcasted_iota(jnp.int32, (tokens, tokens), 1)
        match = (source & (SPAN - 1)) * 6 + lax.shift_right_logical(source, 5) == token
        pick = jnp.where(match, 1.0, 0.0).astype(BF16)
        ordered = jnp.dot(pick, stacked, preferred_element_type=F32)
        patch[...] = ordered[:, 32:96].astype(BF16)
        terms[:, 256:384] = jnp.concatenate([ordered[:, 32:96], ordered[:, 32:96]], axis=1)
        patch_t[...] = ordered.T[32:96].astype(BF16)
        whole[...] = jnp.broadcast_to(jnp.sum(ordered, axis=0, keepdims=True), whole.shape)
        sums[...] = jnp.zeros_like(sums)
        dots[...] = jnp.zeros_like(dots)
        piece[...] = jnp.zeros_like(piece)

    grad = jnp.dot(patch[...], head_weight[...], preferred_element_type=F32)
    normed = (states[...].astype(F32) - stat[:, 0:1]) * stat[:, 128:129]
    weighted = grad * normed
    at = pl.multiple_of(step * STEP, STEP)
    gains[0:1, pl.ds(at, STEP)] = jnp.sum(weighted, axis=0, keepdims=True)
    scale = 1.0 + mods[1:2, :]
    sums[...] += jnp.sum(grad * scale, axis=-1, keepdims=True)
    dots[...] += jnp.sum(weighted * scale, axis=-1, keepdims=True)
    head_input = (normed * scale + mods[0:1, :]).astype(BF16)
    total[:, pl.ds(at, STEP)] = jnp.dot(patch_t[...], head_input, preferred_element_type=F32)

    @pl.when(step == pl.num_programs(0) - 1)
    def _():
        for block in range(40):
            piece[block // 2 : block // 2 + 1, pl.ds((block % 2) * 128, 128)] = gains[
                0:1, block * 128 : (block + 1) * 128
            ]
        extra = jnp.concatenate([piece[...], whole[...], jnp.zeros((32, 128), F32)], axis=1)
        extra = jnp.concatenate([extra, extra], axis=0)
        for out, half in ((load, core[0]), (give, 1 - core[0])):
            rows = total[:, pl.ds(pl.multiple_of(half * HALF, 128), HALF)]
            rows = jnp.concatenate([rows, extra if out is load else extra * 0.0], axis=1)
            out[...] = rows.reshape(64, 24, 128).astype(BF16)
        terms[:, 0:128] = sums[...] * (1.0 / WIDTH)
        terms[:, 128:256] = dots[...] * (1.0 / WIDTH)


def head_sums(core, sent, states, head_weight, mods, stat):
    tokens = states.shape[0]
    fixed = lambda *shape: pl.BlockSpec(shape, lambda i: (0,) * len(shape))
    return pl.pallas_call(
        head_kernel,
        grid=(WIDTH // STEP,),
        in_specs=[
            pl.BlockSpec(memory_space=pltpu.SMEM),
            fixed(SPAN, 8, 128),
            pl.BlockSpec((tokens, STEP), lambda i: (0, i)),
            pl.BlockSpec((64, STEP), lambda i: (0, i)),
            pl.BlockSpec((2, STEP), lambda i: (0, i)),
            fixed(tokens, 256),
        ],
        out_specs=[fixed(64, 24, 128), fixed(64, 24, 128), fixed(tokens, 384)],
        out_shape=[
            jax.ShapeDtypeStruct((64, 24, 128), BF16),
            jax.ShapeDtypeStruct((64, 24, 128), BF16),
            jax.ShapeDtypeStruct((tokens, 384), F32),
        ],
        scratch_shapes=[
            pltpu.VMEM((tokens, 64), BF16),
            pltpu.VMEM((64, tokens), BF16),
            pltpu.VMEM((64, WIDTH), F32),
            pltpu.VMEM((1, WIDTH), F32),
            pltpu.VMEM((32, 128), F32),
            pltpu.VMEM((32, 256), F32),
            pltpu.VMEM((tokens, 128), F32),
            pltpu.VMEM((tokens, 128), F32),
        ],
        compiler_params=pltpu.CompilerParams(vmem_limit_bytes=32 * 1024 * 1024),
        cost_estimate=pl.CostEstimate(
            flops=2 * 2 * 192 * 128 * WIDTH, bytes_accessed=7_000_000, transcendentals=0
        ),
        name="head_sums",
    )(core, sent, states, head_weight, mods, stat)


def combine_kernel(y_high, got, back, whole):
    def add(at, carry):
        for near in range(8):
            carry = carry + got[at * 8 + near].astype(F32)
        return carry

    total = lax.fori_loop(0, 8, add, jnp.zeros((24, 128), F32))
    mine = []
    for y_low in range(2):
        summed = jnp.zeros((24, 128), F32)
        for near in range(16):
            summed = summed + got[y_high[0] * 32 + y_low * 16 + near].astype(F32)
        mine.append(summed)
    row = lax.broadcasted_iota(jnp.int32, (24, 128), 0)
    line = jnp.where(row < 20, total, jnp.where(row < 22, mine[0], pltpu.roll(mine[1], 2, 0)))
    back[...] = jnp.broadcast_to(line.astype(BF16)[None], back.shape)
    whole[...] = jnp.zeros_like(whole)
    whole[0:1] = mine[0][22:23]
    whole[1:2] = mine[1][22:23]


def combine(y_high, got):
    return pl.pallas_call(
        combine_kernel,
        in_specs=[
            pl.BlockSpec(memory_space=pltpu.SMEM),
            pl.BlockSpec(memory_space=pltpu.VMEM),
        ],
        out_specs=[pl.BlockSpec(memory_space=pltpu.VMEM)] * 2,
        out_shape=[
            jax.ShapeDtypeStruct((64, 24, 128), BF16),
            jax.ShapeDtypeStruct((8, 128), F32),
        ],
        compiler_params=pltpu.CompilerParams(vmem_limit_bytes=16 * 1024 * 1024),
        cost_estimate=pl.CostEstimate(
            flops=1_000_000, bytes_accessed=1_600_000, transcendentals=0
        ),
        name="combine",
    )(y_high, got)


def unpack_kernel(place_at, back, theirs, whole, head_weight, weights, mods):
    for source, half in ((back, place_at[0]), (theirs, 1 - place_at[0])):
        rows = source[...].astype(F32).reshape(64, 24 * 128)
        weights[:, pl.ds(pl.multiple_of(half * HALF, 128), HALF)] = rows[:, 0:HALF]
    summed = whole[:, 32:96]
    high = summed.astype(BF16)
    low = (summed - high.astype(F32)).astype(BF16)
    shifts = jnp.dot(high, head_weight[...], preferred_element_type=F32) + jnp.dot(
        low, head_weight[...], preferred_element_type=F32
    )
    for y_low in range(2):
        mods[y_low, 0:1, :] = shifts[y_low : y_low + 1]
    for part in range(20):
        rows = back[place_at[1] * 32 + part].astype(F32)
        for y_low in range(2):
            for near in range(2):
                at = (2 * part + near) * 128
                row = 20 + 2 * y_low + near
                mods[y_low, 1:2, at : at + 128] = rows[row : row + 1]


def unpack(place_at, back, theirs, whole, head_weight):
    return pl.pallas_call(
        unpack_kernel,
        in_specs=[pl.BlockSpec(memory_space=pltpu.SMEM)]
        + [pl.BlockSpec(memory_space=pltpu.VMEM)] * 4,
        out_specs=[pl.BlockSpec(memory_space=pltpu.VMEM)] * 2,
        out_shape=[
            jax.ShapeDtypeStruct((64, WIDTH), F32),
            jax.ShapeDtypeStruct((2, 2, WIDTH), F32),
        ],
        compiler_params=pltpu.CompilerParams(vmem_limit_bytes=24 * 1024 * 1024),
        cost_estimate=pl.CostEstimate(
            flops=10_000_000, bytes_accessed=3_000_000, transcendentals=0
        ),
        name="unpack",
    )(place_at, back, theirs, whole, head_weight)


def hidden_kernel(terms, states, head_weight, mods, stat, out):
    patch = terms[:, 256:320].astype(BF16)
    grad = jnp.dot(patch, head_weight[...], preferred_element_type=F32)
    inv_std = stat[:, 128:129]
    normed = (states[...].astype(F32) - stat[:, 0:1]) * inv_std
    scaled = grad * (1.0 + mods[1:2, :])
    out[...] = ((scaled - terms[:, 0:1] - normed * terms[:, 128:129]) * inv_std).astype(BF16)


def hidden_grads(terms, states, head_weight, mods, stat):
    tokens = states.shape[0]
    fixed = lambda *shape: pl.BlockSpec(shape, lambda i: (0, 0))
    return pl.pallas_call(
        hidden_kernel,
        grid=(WIDTH // STEP,),
        in_specs=[
            fixed(tokens, 384),
            pl.BlockSpec((tokens, STEP), lambda i: (0, i)),
            pl.BlockSpec((64, STEP), lambda i: (0, i)),
            pl.BlockSpec((2, STEP), lambda i: (0, i)),
            fixed(tokens, 256),
        ],
        out_specs=pl.BlockSpec((tokens, STEP), lambda i: (0, i)),
        out_shape=jax.ShapeDtypeStruct((tokens, WIDTH), BF16),
        compiler_params=pltpu.CompilerParams(vmem_limit_bytes=LARGE),
        cost_estimate=pl.CostEstimate(
            flops=2 * 192 * 128 * WIDTH, bytes_accessed=6_000_000, transcendentals=0
        ),
        name="hidden_grads",
    )(terms, states, head_weight, mods, stat)


def channel_order(core, x, z, y_low):
    at = jnp.arange(CH, dtype=jnp.int32)
    first, second, rel, inner = at // 96, (at // 24) % 4, (at // 12) % 2, at % 12
    x_at = (x + jnp.where(core == 0, second, first)) % 4
    z_at = (z + jnp.where(core == 0, first, second)) % 4
    channel = 12 * ((y_low ^ rel) * 16 + x_at * 4 + z_at) + inner
    return (channel[:, None] == jnp.arange(CH, dtype=jnp.int32)[None, :]).astype(BF16)


def sum_kernel(first, second, third, fourth, *outs):
    rows = outs[0].shape[1]
    for tap in range(first.shape[0]):
        total = (first[tap].astype(F32) + second[tap].astype(F32)) + (
            third[tap].astype(F32) + fourth[tap].astype(F32)
        )
        for part, out in enumerate(outs):
            out[tap] = total[part * rows : (part + 1) * rows].astype(BF16)


def sum_parts(terms, count):
    taps, rows, _ = terms[0].shape
    block = lambda height: pl.BlockSpec((taps // 2, height, CH), lambda i: (i, 0, 0))
    return pl.pallas_call(
        sum_kernel,
        grid=(2,),
        in_specs=[block(rows)] * 4,
        out_specs=[block(rows // count)] * count,
        out_shape=[jax.ShapeDtypeStruct((taps, rows // count, CH), BF16)] * count,
        compiler_params=pltpu.CompilerParams(vmem_limit_bytes=LARGE),
        cost_estimate=pl.CostEstimate(flops=1, bytes_accessed=1, transcendentals=0),
        name="sum_parts",
    )(*terms)


def last_kernel(same, far, upper, lower, out):
    out[...] = (same[...].astype(F32) + far[...].astype(F32)) + (
        upper[...].astype(F32) + lower[...].astype(F32)
    )


def last_sum(*terms):
    return pl.pallas_call(
        last_kernel,
        in_specs=[IN_VMEM] * 4,
        out_specs=IN_VMEM,
        out_shape=jax.ShapeDtypeStruct(terms[0].shape, F32),
        compiler_params=pltpu.CompilerParams(vmem_limit_bytes=8 * 1024 * 1024),
        cost_estimate=pl.CostEstimate(flops=1, bytes_accessed=1, transcendentals=0),
        name="last_sum",
    )(*terms)


def added(*terms):
    return functools.reduce(lambda a, b: a + b, [term.astype(F32) for term in terms])


def local(
    features, pixel_grad, frame_list, conv_weight, in_weight, last_hidden, modulation, head_weight
):
    clips, frames, rows_here, columns, _ = features.shape
    clip = lax.axis_index("clip")
    tile = lax.axis_index("tile")
    _, x, z, core = place(clip, tile)
    y_low = tile // 16

    up = [(i, i + 1) for i in range(31)]
    down = [(i + 1, i) for i in range(31)]
    border = [
        jnp.transpose(pixel_grad[:, :, row], (2, 0, 1, 3)).reshape(columns, SPAN, CH)
        for row in (0, 1)
    ]
    low = lax.ppermute(border[1], "tile", up)
    high = lax.ppermute(border[0], "tile", down)

    scored = jnp.any(
        frame_list[:, None, :] == jnp.arange(frames, dtype=jnp.int32)[None, :, None], axis=-1
    ).astype(BF16)
    keep = jnp.broadcast_to(scored.reshape(SPAN, 1), (SPAN, CH))
    masked = pixel_grad * scored[:, :, None, None, None]
    own = jnp.transpose(masked, (2, 3, 0, 1, 4)).reshape(rows_here, columns, SPAN, CH)
    feats = jnp.transpose(features, (2, 3, 0, 1, 4)).reshape(rows_here, columns, SPAN, CH)
    own2 = lax.ppermute(own, BOTH, OTHER_CORE)
    acts = jax.nn.silu(feats.astype(F32)).astype(BF16)
    acts2 = lax.ppermute(acts, BOTH, OTHER_CORE)
    keep2 = lax.ppermute(keep, BOTH, OTHER_CORE)
    low2 = lax.ppermute(low, BOTH, OTHER_CORE)
    high2 = lax.ppermute(high, BOTH, OTHER_CORE)

    mods = lax.dynamic_index_in_dim(modulation, y_low, 0, keepdims=False)
    head_t = head_weight.T
    core_at = core.astype(jnp.int32).reshape(1)
    y_high = (clip // 2).astype(jnp.int32).reshape(1)
    order = channel_order(core, x, z, y_low)
    parts = weight_grad(
        core_at, own, low, high, keep, acts, own2, low2, high2, keep2, acts2, order
    )
    moved = [lax.ppermute(parts[k], BOTH, along(0, k)) for k in (1, 2, 3)]

    low, high, _ = lax.optimization_barrier((low, high, parts))
    sent = input_grad(own, low, high, keep, feats, conv_weight, in_weight)
    states, _ = lax.optimization_barrier((last_hidden, sent))
    stat = stats(states)
    sent = lax.all_to_all(sent, "tile", 0, 0, tiled=True)
    moved, _ = lax.optimization_barrier((moved, stat))
    rows = sum_parts([parts[0], *moved], 4)
    sent, rows = lax.optimization_barrier((sent, rows))
    load, give, terms = head_sums(core_at, sent, last_hidden, head_t, mods, stat)
    taken = lax.ppermute(give, BOTH, OTHER_CORE)
    load = added(load, taken).astype(BF16)
    got = lax.all_to_all(load, BOTH, 0, 0, tiled=True, axis_index_groups=SAME_CORE)
    moved = [lax.ppermute(rows[k], BOTH, along(1, k)) for k in (1, 2, 3)]
    got, rows = lax.optimization_barrier((got, rows))

    back, whole_patch = combine(y_high, got)
    moved, _ = lax.optimization_barrier((moved, back))
    same, flipped = sum_parts([rows[0], *moved], 2)
    terms, same, flipped = lax.optimization_barrier((terms, same, flipped))
    hidden_grad = hidden_grads(terms, last_hidden, head_t, mods, stat)
    far = lax.ppermute(same, BOTH, along_y(2))
    upper = lax.ppermute(flipped, BOTH, along_y(1))
    lower = lax.ppermute(flipped, BOTH, along_y(3))
    back = lax.all_to_all(back, BOTH, 0, 0, tiled=True, axis_index_groups=SAME_CORE)
    share = last_sum(same, far, upper, lower)
    share, hidden_grad, _ = lax.optimization_barrier((share, hidden_grad, back))
    other = lax.ppermute(back, BOTH, OTHER_CORE)
    weights, modulation_grad = unpack(
        jnp.concatenate([core_at, y_high]), back, other, whole_patch, head_t
    )

    theirs = lax.ppermute(share, BOTH, OTHER_CORE)
    first = jnp.where(core == 0, share, theirs)
    second = jnp.where(core == 0, theirs, share)
    conv_weight_grad = jnp.concatenate([first, second[10:], second[:9]], axis=0)
    return (
        hidden_grad, weights.T, modulation_grad, conv_weight_grad.reshape(3, 3, 3, 12, CH)
    )


def solution(mesh):
    return jax.shard_map(
        local,
        mesh=mesh,
        in_specs=(
            P("clip", None, "tile", None, None),
            P("clip", None, "tile", None, None),
            P("clip", None),
            P(),
            P(),
            P(("clip", "tile"), None),
            P("clip", None, None),
            P(),
        ),
        out_specs=(
            P(("clip", "tile"), None),
            P(),
            P("clip", None, None),
            P(None, None, None, "tile", None),
        ),
        check_vma=False,
    )
```

profile of v0, /device:TPU:1, one launch (start us, length us, event | category | flops | bytes accessed | tf_op | source)
XLA Modules:
  0.0 125.1 jit_solution(4411808365498277160)
XLA Ops:
  0.6 0.0 copy-start
  0.6 2.3 %fusion.27 = (bf16[2,16,1,12,384]{4,2,3,1,0:T(2,128)(2,1)S(1)}, bf16[2,16,1,12,384]{4,2,3,1,0:T(2,128)(2,1)S(1)}) fusion(bf16[2,16,2,12,384]{4,2,3,1,0:T(2,128)(2,1)} %param.9), kind=kLoop, calls=%fused_computation.60 | loop fusion | bytes 1179648 | tf_op jit(solution)/shard_map/slice | solution.py:574
  3.0 0.0 copy-start.24
  3.0 0.0 copy-start.8
  3.0 4.5 %collective-permute-start = (bf16[12,32,384]{2,1,0:T(8,128)(2,1)S(1)}, bf16[12,32,384]{2,1,0:T(8,128)(2,1)S(1)}, u32[]{:S(2)}, u32[]{:S(2)}) collective-permute-start(bf16[12,32,384]{2,1,0:T(8,128)(2,1)S(1)} %bitcast.35), channel_id=1, source_target_pairs={{0,1},{1,2},{2,3},{3,4},{4,5},{5,6},{6,7},{7,8},{8,9},{9,10},{10,1... | collective-permute-start | bytes 884744 | tf_op jit(solution)/shard_map/ppermute | solution.py:577
  7.6 1.3 %collective-permute-start.1 = (bf16[12,32,384]{2,1,0:T(8,128)(2,1)S(1)}, bf16[12,32,384]{2,1,0:T(8,128)(2,1)}, u32[]{:S(2)}, u32[]{:S(2)}) collective-permute-start(bf16[12,32,384]{2,1,0:T(8,128)(2,1)S(1)} %bitcast.34), channel_id=1, source_target_pairs={{1,0},{2,1},{3,2},{4,3},{5,4},{6,5},{7,6},{8,7},{9,8},{10,9},{11,1... | collective-permute-start | bytes 884744 | tf_op jit(solution)/shard_map/ppermute | solution.py:578
  8.9 0.1 fusion.5
  9.1 0.6 multiply_bitcast_fusion
  9.7 0.1 copy.22
  9.8 1.0 collective-permute-start.2
  10.8 0.1 copy.27
  10.9 0.4 fusion.3.acts
  11.3 0.4 collective-permute-start.6
  11.7 0.1 reshape.136
  11.7 0.1 broadcast_in_dim.2.keep
  11.8 0.3 collective-permute-start.5
  12.1 1.1 collective-permute-done.low
  13.2 1.5 %collective-permute-start.3 = (bf16[12,32,384]{2,1,0:T(8,128)(2,1)S(1)}, bf16[12,32,384]{2,1,0:T(8,128)(2,1)}, u32[]{:S(2)}, u32[]{:S(2)}) collective-permute-start(bf16[12,32,384]{2,1,0:T(8,128)(2,1)S(1)} %collective-permute-done.low), channel_id=1, source_target_pairs={{0,32},{1,33},{2,34},{3,35},{4,36},{5,37},{6,38},{7,39},{8,40},{9,... | collective-permute-start | bytes 884744 | tf_op jit(solution)/shard_map/ppermute | solution.py:591
  14.7 2.8 %collective-permute-done.1.high = bf16[12,32,384]{2,1,0:T(8,128)(2,1)} collective-permute-done((bf16[12,32,384]{2,1,0:T(8,128)(2,1)S(1)}, bf16[12,32,384]{2,1,0:T(8,128)(2,1)}, u32[]{:S(2)}, u32[]{:S(2)}) %collective-permute-start.1) | collective-permute-done | bytes 294944 | tf_op jit(solution)/shard_map/ppermute | solution.py:578
  17.5 1.7 %collective-permute-start.4 = (bf16[12,32,384]{2,1,0:T(8,128)(2,1)}, bf16[12,32,384]{2,1,0:T(8,128)(2,1)S(1)}, u32[]{:S(2)}, u32[]{:S(2)}) collective-permute-start(bf16[12,32,384]{2,1,0:T(8,128)(2,1)} %collective-permute-done.1.high), channel_id=1, source_target_pairs={{0,32},{1,33},{2,34},{3,35},{4,36},{5,37},{6,38},{7,39},{8,40},{9,... | collective-permute-start | bytes 884744 | tf_op jit(solution)/shard_map/ppermute | solution.py:592
  19.2 0.8 fusion.4.order
  20.1 0.5 collective-permute-done.4.high2
  20.6 0.0 copy-done.23
  20.7 0.2 copy-done.17
  20.9 0.5 copy-done.19
  21.3 12.5 %weight_grad.1 = (bf16[14,96,384]{2,1,0:T(8,128)(2,1)}, bf16[14,96,384]{2,1,0:T(8,128)(2,1)}, bf16[14,96,384]{2,1,0:T(8,128)(2,1)}, bf16[14,96,384]{2,1,0:T(8,128)(2,1)}) custom-call(s32[1]{0:T(128)} %bitcast.core, bf16[2,12,32,384]{3,2,1,0:T(8,128)(2,1)} %bitcast.32, bf16[12,32,384]{2,1,0:T(8,128)(2,1)} %copy-done.18, ...), custom_call_target="tpu_custom_call" | custom-call | flops 6341787648 | bytes 12000000 | tf_op jit(solution)/shard_map/weight_grad/pallas_call | solution.py:245
  33.8 1.3 %collective-permute-start.7 = (bf16[14,96,384]{2,1,0:T(8,128)(2,1)}, bf16[14,96,384]{2,1,0:T(8,128)(2,1)}, u32[]{:S(2)}, u32[]{:S(2)}) collective-permute-start(bf16[14,96,384]{2,1,0:T(8,128)(2,1)} %get-tuple-element.43), channel_id=1, source_target_pairs={{0,1},{1,2},{2,3},{3,0},{4,5},{5,6},{6,7},{7,4},{8,9},{9,10},{10,1... | collective-permute-start | bytes 3096584 | tf_op jit(solution)/shard_map/ppermute | solution.py:602
  35.1 2.5 %collective-permute-start.8 = (bf16[14,96,384]{2,1,0:T(8,128)(2,1)}, bf16[14,96,384]{2,1,0:T(8,128)(2,1)}, u32[]{:S(2)}, u32[]{:S(2)}) collective-permute-start(bf16[14,96,384]{2,1,0:T(8,128)(2,1)} %get-tuple-element.44), channel_id=1, source_target_pairs={{0,2},{1,3},{2,0},{3,1},{4,6},{5,7},{6,4},{7,5},{8,10},{9,11},{10,... | collective-permute-start | bytes 3096584 | tf_op jit(solution)/shard_map/ppermute | solution.py:602
  37.6 1.1 collective-permute-start.9
  38.7 12.4 %input_grad.1 = f32[32,8,128]{2,1,0:T(8,128)} custom-call(bf16[2,12,32,384]{3,2,1,0:T(8,128)(2,1)} %bitcast.33, bf16[12,32,384]{2,1,0:T(8,128)(2,1)} %copy-done.18, bf16[12,32,384]{2,1,0:T(8,128)(2,1)} %collective-permute-done.1.high, bf16[32,384]{1,0:T(8,128)(2,1)} %copy-done.16, bf16[2,12,32,384]{3,2,1,0:T(8,128)(2,1)} %bitcast.28, ...), custom_call_target="tpu_custom_call" | custom-call | flops 6115295232 | bytes 12000000 | tf_op jit(solution)/shard_map/input_grad/pallas_call | solution.py:167
  51.2 7.9 %all-to-all-start = ((f32[32,8,128]{2,1,0:T(8,128)}), f32[32,8,128]{2,1,0:T(8,128)S(1)}, u32[]{:S(2)}, u32[]{:S(2)}) async-start(f32[32,8,128]{2,1,0:T(8,128)} %input_grad.1), calls=%async_computation | async-start | bytes 262144 | tf_op jit(solution)/shard_map/all_to_all | solution.py:608
  59.1 1.8 %token_stats.1.stat = f32[192,256]{1,0:T(8,128)S(1)} custom-call(bf16[192,5120]{1,0:T(8,128)(2,1)S(1)} %copy-done.1), custom_call_target="tpu_custom_call" | custom-call | flops 1 | bytes 1 | tf_op jit(solution)/shard_map/token_stats/pallas_call | solution.py:283
  61.0 0.3 collective-permute-done.8.third
  61.2 3.1 %sum_parts.2 = (bf16[14,24,384]{2,1,0:T(8,128)(2,1)}, bf16[14,24,384]{2,1,0:T(8,128)(2,1)}, bf16[14,24,384]{2,1,0:T(8,128)(2,1)}, bf16[14,24,384]{2,1,0:T(8,128)(2,1)}) custom-call(bf16[14,96,384]{2,1,0:T(8,128)(2,1)} %get-tuple-element.42.first, bf16[14,96,384]{2,1,0:T(8,128)(2,1)} %collective-permute-done.7.second, ...), custom_call_target="tpu_custom_call" | custom-call | flops 1 | bytes 1 | tf_op jit(solution)/shard_map/sum_parts/pallas_call | solution.py:528
  64.4 3.8 %all-to-all-done.sent = f32[32,8,128]{2,1,0:T(8,128)S(1)} async-done(((f32[32,8,128]{2,1,0:T(8,128)}), f32[32,8,128]{2,1,0:T(8,128)S(1)}, u32[]{:S(2)}, u32[]{:S(2)}) %all-to-all-start) | async-done | bytes 131104 | tf_op jit(solution)/shard_map/all_to_all | solution.py:608
  68.2 3.4 %head_sums.1 = (bf16[64,24,128]{2,1,0:T(8,128)(2,1)S(1)}, bf16[64,24,128]{2,1,0:T(8,128)(2,1)S(1)}, f32[192,384]{1,0:T(8,128)S(1)}) custom-call(s32[1]{0:T(128)} %bitcast.core, f32[32,8,128]{2,1,0:T(8,128)S(1)} %all-to-all-done.sent, bf16[192,5120]{1,0:T(8,128)(2,1)S(1)} %copy-done.1, bf16[64,5120]{1,0:T(8,128)(2,1)S(1)} %bitcast.26, ...), custom_call_target="tpu_custom_call" | custom-call | flops 503316480 | bytes 7000000 | tf_op jit(solution)/shard_map/head_sums/pallas_call | solution.py:359
  71.6 0.7 copy-done.6
  72.3 0.9 collective-permute-start.10
  73.1 1.3 %collective-permute-done.10 = bf16[64,24,128]{2,1,0:T(8,128)(2,1)S(1)} collective-permute-done((bf16[64,24,128]{2,1,0:T(8,128)(2,1)S(1)}, bf16[64,24,128]{2,1,0:T(8,128)(2,1)S(1)}, u32[]{:S(2)}, u32[]{:S(2)}) %collective-permute-start.10) | collective-permute-done | bytes 393248 | tf_op jit(solution)/shard_map/ppermute | solution.py:613
  74.5 0.8 add_convert_fusion
  75.3 10.5 %all-to-all-start.1 = ((bf16[64,24,128]{2,1,0:T(8,128)(2,1)}), bf16[64,24,128]{2,1,0:T(8,128)(2,1)S(1)}, u32[]{:S(2)}, u32[]{:S(2)}) async-start(bf16[64,24,128]{2,1,0:T(8,128)(2,1)} %add_convert_fusion), calls=%async_computation.1 | async-start | bytes 786432 | tf_op jit(solution)/shard_map/all_to_all | solution.py:615
  85.9 1.1 collective-permute-start.11
  87.0 2.4 %collective-permute-start.12 = (bf16[14,24,384]{2,1,0:T(8,128)(2,1)S(1)}, bf16[14,24,384]{2,1,0:T(8,128)(2,1)S(1)}, u32[]{:S(2)}, u32[]{:S(2)}) collective-permute-start(bf16[14,24,384]{2,1,0:T(8,128)(2,1)S(1)} %copy-done.21), channel_id=1, source_target_pairs={{0,8},{1,9},{2,10},{3,11},{4,12},{5,13},{6,14},{7,15},{8,0},{9,1},... | collective-permute-start | bytes 774152 | tf_op jit(solution)/shard_map/ppermute | solution.py:616
  89.4 1.2 collective-permute-start.13
  90.6 6.3 %all-to-all-done.1.got = bf16[64,24,128]{2,1,0:T(8,128)(2,1)S(1)} async-done(((bf16[64,24,128]{2,1,0:T(8,128)(2,1)}), bf16[64,24,128]{2,1,0:T(8,128)(2,1)S(1)}, u32[]{:S(2)}, u32[]{:S(2)}) %all-to-all-start.1) | async-done | bytes 393248 | tf_op jit(solution)/shard_map/all_to_all | solution.py:615
  96.8 0.9 combine.1
  97.7 4.9 %all-to-all-start.2 = ((bf16[64,24,128]{2,1,0:T(8,128)(2,1)}), bf16[64,24,128]{2,1,0:T(8,128)(2,1)S(1)}, u32[]{:S(2)}, u32[]{:S(2)}) async-start(bf16[64,24,128]{2,1,0:T(8,128)(2,1)} %get-tuple-element.66), calls=%async_computation.2 | async-start | bytes 786432 | tf_op jit(solution)/shard_map/all_to_all | solution.py:627
  102.7 0.7 copy-done.13
  103.4 0.1 copy-done.14
  103.5 0.7 copy-done.15
  104.2 2.0 %sum_parts.3 = (bf16[14,12,384]{2,1,0:T(8,128)(2,1)}, bf16[14,12,384]{2,1,0:T(8,128)(2,1)}) custom-call(bf16[14,24,384]{2,1,0:T(8,128)(2,1)} %get-tuple-element.64.first, bf16[14,24,384]{2,1,0:T(8,128)(2,1)} %copy-done.13, bf16[14,24,384]{2,1,0:T(8,128)(2,1)} %copy-done.14, bf16[14,24,384]{2,1,0:T(8,128)(2,1)} %copy-done.15), custom_call_target="tpu_custom_call" | custom-call | flops 1 | bytes 1 | tf_op jit(solution)/shard_map/sum_parts/pallas_call | solution.py:528
  106.2 2.7 %collective-permute-start.14 = (bf16[14,12,384]{2,1,0:T(8,128)(2,1)}, bf16[14,12,384]{2,1,0:T(8,128)(2,1)S(1)}, u32[]{:S(2)}, u32[]{:S(2)}) collective-permute-start(bf16[14,12,384]{2,1,0:T(8,128)(2,1)} %get-tuple-element.72.same), channel_id=1, source_target_pairs={{0,64},{1,65},{2,66},{3,67},{4,68},{5,69},{6,70},{7,71},{8,72},{9,... | collective-permute-start | bytes 387080 | tf_op jit(solution)/shard_map/ppermute | solution.py:624
  108.9 0.4 collective-permute-start.15
  109.3 2.3 %collective-permute-start.16 = (bf16[14,12,384]{2,1,0:T(8,128)(2,1)}, bf16[14,12,384]{2,1,0:T(8,128)(2,1)S(1)}, u32[]{:S(2)}, u32[]{:S(2)}) collective-permute-start(bf16[14,12,384]{2,1,0:T(8,128)(2,1)} %get-tuple-element.73), channel_id=1, source_target_pairs={{0,80},{1,81},{2,82},{3,83},{4,84},{5,85},{6,86},{7,87},{8,88},{9,... | collective-permute-start | bytes 387080 | tf_op jit(solution)/shard_map/ppermute | solution.py:626
  111.6 4.8 %hidden_grads.1 = bf16[192,5120]{1,0:T(8,128)(2,1)} custom-call(f32[192,384]{1,0:T(8,128)} %copy-done.6, bf16[192,5120]{1,0:T(8,128)(2,1)} %states.4, bf16[64,5120]{1,0:T(8,128)(2,1)} %bitcast.25, f32[2,5120]{1,0:T(2,128)} %copy-done.5, f32[192,256]{1,0:T(8,128)} %copy-done.4), custom_call_target="tpu_custom_call" | custom-call | flops 251658240 | bytes 6000000 | tf_op jit(solution)/shard_map/hidden_grads/pallas_call | solution.py:486
  116.4 2.6 %collective-permute-done.15.upper = bf16[14,12,384]{2,1,0:T(8,128)(2,1)S(1)} collective-permute-done((bf16[14,12,384]{2,1,0:T(8,128)(2,1)}, bf16[14,12,384]{2,1,0:T(8,128)(2,1)S(1)}, u32[]{:S(2)}, u32[]{:S(2)}) %collective-permute-start.15) | collective-permute-done | bytes 129056 | tf_op jit(solution)/shard_map/ppermute | solution.py:625
  119.0 0.1 last_sum.1
  119.1 1.1 collective-permute-start.18
  120.2 0.1 collective-permute-start.17
  120.3 0.1 pad_add_fusion.place_at
  120.4 1.1 collective-permute-done.18
  121.6 0.9 pad_maximum_fusion
  122.5 0.4 copy-done.3
  122.8 2.3 %unpack.1 = (f32[64,5120]{1,0:T(8,128)}, f32[2,2,5120]{2,1,0:T(2,128)}) custom-call(s32[2]{0:T(128)S(1)} %pad_add_fusion.place_at, bf16[64,24,128]{2,1,0:T(8,128)(2,1)S(1)} %all-to-all-done.2.back, bf16[64,24,128]{2,1,0:T(8,128)(2,1)S(1)} %collective-permute-done.17.theirs, f32[8,128]{1,0:T(8,128)S(1)} %get-tuple-element.76.whole, bf16[64,5120]{1,0:T(8,128)(2,1)S(1)} %bitcast.27), custom_call_target="tpu_custom_call" | custom-call | flops 10000000 | bytes 3000000 | tf_op jit(solution)/shard_map/unpack/pallas_call | solution.py:457
  (60 shorter events, 0.3 us)
Async XLA Ops:
  0.6 58.4 %copy-start = (f32[2,2,5120]{2,1,0:T(2,128)S(1)}, f32[2,2,5120]{2,1,0:T(2,128)}, u32[]{:S(2)}) copy-start(f32[2,2,5120]{2,1,0:T(2,128)} %param.14) | copy-start | bytes 245764
  3.0 6.0 %copy-start.24 = (s32[2,16]{1,0:T(2,128)S(1)}, s32[2,16]{1,0:T(2,128)}, u32[]{:S(2)}) copy-start(s32[2,16]{1,0:T(2,128)} %param.10) | copy-start | bytes 388
  3.0 6.1 %copy-start.8 = (bf16[2,16,2,12,384]{4,2,3,1,0:T(2,128)(2,1)S(1)}, bf16[2,16,2,12,384]{4,2,3,1,0:T(2,128)(2,1)}, u32[]{:S(2)}) copy-start(bf16[2,16,2,12,384]{4,2,3,1,0:T(2,128)(2,1)} %param.9) | copy-start | bytes 1769476
  3.0 10.2 %collective-permute-start = (bf16[12,32,384]{2,1,0:T(8,128)(2,1)S(1)}, bf16[12,32,384]{2,1,0:T(8,128)(2,1)S(1)}, u32[]{:S(2)}, u32[]{:S(2)}) collective-permute-start(bf16[12,32,384]{2,1,0:T(8,128)(2,1)S(1)} %bitcast.35), channel_id=1, source_target_pairs={{0,1},{1,2},{2,3},{3,4},{4,5},{5,6},{6,7},{7,8},{8,9},{9,10},{10,1... | collective-permute-start | bytes 884744 | tf_op jit(solution)/shard_map/ppermute | solution.py:577
  7.6 9.9 %collective-permute-start.1 = (bf16[12,32,384]{2,1,0:T(8,128)(2,1)S(1)}, bf16[12,32,384]{2,1,0:T(8,128)(2,1)}, u32[]{:S(2)}, u32[]{:S(2)}) collective-permute-start(bf16[12,32,384]{2,1,0:T(8,128)(2,1)S(1)} %bitcast.34), channel_id=1, source_target_pairs={{1,0},{2,1},{3,2},{4,3},{5,4},{6,5},{7,6},{8,7},{9,8},{10,9},{11,1... | collective-permute-start | bytes 884744 | tf_op jit(solution)/shard_map/ppermute | solution.py:578
  9.0 1.7 %copy-start.10 = (bf16[2,16,2,12,384]{4,2,3,1,0:T(2,128)(2,1)S(1)}, bf16[2,16,2,12,384]{4,2,3,1,0:T(2,128)(2,1)}, u32[]{:S(2)}) copy-start(bf16[2,16,2,12,384]{4,2,3,1,0:T(2,128)(2,1)} %param.8) | copy-start | bytes 1769476
  9.7 1.5 %copy-start.11 = (bf16[2,12,2,16,384]{4,3,2,1,0:T(8,128)(2,1)}, bf16[2,12,2,16,384]{4,3,2,1,0:T(8,128)(2,1)S(1)}, u32[]{:S(2)}) copy-start(bf16[2,12,2,16,384]{4,3,2,1,0:T(8,128)(2,1)S(1)} %copy.22) | copy-start | bytes 1769476
  9.8 10.3 %collective-permute-start.2 = (bf16[2,12,32,384]{3,2,1,0:T(8,128)(2,1)S(1)}, bf16[2,12,32,384]{3,2,1,0:T(8,128)(2,1)S(1)}, u32[]{:S(2)}, u32[]{:S(2)}) collective-permute-start(bf16[2,12,32,384]{3,2,1,0:T(8,128)(2,1)S(1)} %bitcast.31), channel_id=1, source_target_pairs={{0,32},{1,33},{2,34},{3,35},{4,36},{5,37},{6,38},{7,39},{8,40},{9,... | collective-permute-start | bytes 1769480 | tf_op jit(solution)/shard_map/ppermute | solution.py:587
  10.9 23.0 %copy-start.9 = (bf16[2,12,2,16,384]{4,3,2,1,0:T(8,128)(2,1)}, bf16[2,12,2,16,384]{4,3,2,1,0:T(8,128)(2,1)S(1)}, u32[]{:S(2)}) copy-start(bf16[2,12,2,16,384]{4,3,2,1,0:T(8,128)(2,1)S(1)} %copy.27) | copy-start | bytes 1769476
  11.3 9.3 %copy-start.12 = (bf16[2,12,32,384]{3,2,1,0:T(8,128)(2,1)}, bf16[2,12,32,384]{3,2,1,0:T(8,128)(2,1)S(1)}, u32[]{:S(2)}) copy-start(bf16[2,12,32,384]{3,2,1,0:T(8,128)(2,1)S(1)} %fusion.3.acts) | copy-start | bytes 1769476
  11.3 9.3 %collective-permute-start.6 = (bf16[2,12,32,384]{3,2,1,0:T(8,128)(2,1)S(1)}, bf16[2,12,32,384]{3,2,1,0:T(8,128)(2,1)}, u32[]{:S(2)}, u32[]{:S(2)}) collective-permute-start(bf16[2,12,32,384]{3,2,1,0:T(8,128)(2,1)S(1)} %fusion.3.acts), channel_id=1, source_target_pairs={{0,32},{1,33},{2,34},{3,35},{4,36},{5,37},{6,38},{7,39},{8,40},{9,... | collective-permute-start | bytes 1769480 | tf_op jit(solution)/shard_map/ppermute | solution.py:589
  11.8 8.8 %copy-start.16 = (bf16[32,384]{1,0:T(8,128)(2,1)}, bf16[32,384]{1,0:T(8,128)(2,1)S(1)}, u32[]{:S(2)}) copy-start(bf16[32,384]{1,0:T(8,128)(2,1)S(1)} %broadcast_in_dim.2.keep) | copy-start | bytes 73732
  11.8 8.2 %collective-permute-start.5 = (bf16[32,384]{1,0:T(8,128)(2,1)S(1)}, bf16[32,384]{1,0:T(8,128)(2,1)S(1)}, u32[]{:S(2)}, u32[]{:S(2)}) collective-permute-start(bf16[32,384]{1,0:T(8,128)(2,1)S(1)} %broadcast_in_dim.2.keep), channel_id=1, source_target_pairs={{0,32},{1,33},{2,34},{3,35},{4,36},{5,37},{6,38},{7,39},{8,40},{9,... | collective-permute-start | bytes 73736 | tf_op jit(solution)/shard_map/ppermute | solution.py:590
  13.2 7.4 %copy-start.18 = (bf16[12,32,384]{2,1,0:T(8,128)(2,1)}, bf16[12,32,384]{2,1,0:T(8,128)(2,1)S(1)}, u32[]{:S(2)}) copy-start(bf16[12,32,384]{2,1,0:T(8,128)(2,1)S(1)} %collective-permute-done.low) | copy-start | bytes 884740
  13.2 6.9 %collective-permute-start.3 = (bf16[12,32,384]{2,1,0:T(8,128)(2,1)S(1)}, bf16[12,32,384]{2,1,0:T(8,128)(2,1)}, u32[]{:S(2)}, u32[]{:S(2)}) collective-permute-start(bf16[12,32,384]{2,1,0:T(8,128)(2,1)S(1)} %collective-permute-done.low), channel_id=1, source_target_pairs={{0,32},{1,33},{2,34},{3,35},{4,36},{5,37},{6,38},{7,39},{8,40},{9,... | collective-permute-start | bytes 884744 | tf_op jit(solution)/shard_map/ppermute | solution.py:591
  17.5 3.1 %collective-permute-start.4 = (bf16[12,32,384]{2,1,0:T(8,128)(2,1)}, bf16[12,32,384]{2,1,0:T(8,128)(2,1)S(1)}, u32[]{:S(2)}, u32[]{:S(2)}) collective-permute-start(bf16[12,32,384]{2,1,0:T(8,128)(2,1)} %collective-permute-done.1.high), channel_id=1, source_target_pairs={{0,32},{1,33},{2,34},{3,35},{4,36},{5,37},{6,38},{7,39},{8,40},{9,... | collective-permute-start | bytes 884744 | tf_op jit(solution)/shard_map/ppermute | solution.py:592
  20.1 0.6 copy-start.23
  20.1 0.8 copy-start.17
  20.6 0.7 copy-start.19
  33.8 27.1 %collective-permute-start.7 = (bf16[14,96,384]{2,1,0:T(8,128)(2,1)}, bf16[14,96,384]{2,1,0:T(8,128)(2,1)}, u32[]{:S(2)}, u32[]{:S(2)}) collective-permute-start(bf16[14,96,384]{2,1,0:T(8,128)(2,1)} %get-tuple-element.43), channel_id=1, source_target_pairs={{0,1},{1,2},{2,3},{3,0},{4,5},{5,6},{6,7},{7,4},{8,9},{9,10},{10,1... | collective-permute-start | bytes 3096584 | tf_op jit(solution)/shard_map/ppermute | solution.py:602
  35.1 26.1 %collective-permute-start.8 = (bf16[14,96,384]{2,1,0:T(8,128)(2,1)}, bf16[14,96,384]{2,1,0:T(8,128)(2,1)}, u32[]{:S(2)}, u32[]{:S(2)}) collective-permute-start(bf16[14,96,384]{2,1,0:T(8,128)(2,1)} %get-tuple-element.44), channel_id=1, source_target_pairs={{0,2},{1,3},{2,0},{3,1},{4,6},{5,7},{6,4},{7,5},{8,10},{9,11},{10,... | collective-permute-start | bytes 3096584 | tf_op jit(solution)/shard_map/ppermute | solution.py:602
  37.6 23.7 %collective-permute-start.9 = (bf16[14,96,384]{2,1,0:T(8,128)(2,1)}, bf16[14,96,384]{2,1,0:T(8,128)(2,1)}, u32[]{:S(2)}, u32[]{:S(2)}) collective-permute-start(bf16[14,96,384]{2,1,0:T(8,128)(2,1)} %get-tuple-element.45), channel_id=1, source_target_pairs={{0,3},{1,0},{2,1},{3,2},{4,7},{5,4},{6,5},{7,6},{8,11},{9,8},{10,9... | collective-permute-start | bytes 3096584 | tf_op jit(solution)/shard_map/ppermute | solution.py:602
  38.7 20.3 %copy-start.1 = (bf16[192,5120]{1,0:T(8,128)(2,1)S(1)}, bf16[192,5120]{1,0:T(8,128)(2,1)}, u32[]{:S(2)}) copy-start(bf16[192,5120]{1,0:T(8,128)(2,1)} %states.4) | copy-start | bytes 5898244
  51.2 17.0 %all-to-all-start = ((f32[32,8,128]{2,1,0:T(8,128)}), f32[32,8,128]{2,1,0:T(8,128)S(1)}, u32[]{:S(2)}, u32[]{:S(2)}) async-start(f32[32,8,128]{2,1,0:T(8,128)} %input_grad.1), calls=%async_computation | async-start | bytes 262144 | tf_op jit(solution)/shard_map/all_to_all | solution.py:608
  59.1 9.1 %copy-start.5 = (f32[2,5120]{1,0:T(2,128)}, f32[2,5120]{1,0:T(2,128)S(1)}, u32[]{:S(2)}) copy-start(f32[2,5120]{1,0:T(2,128)S(1)} %dynamic-slice_bitcast_fusion.mods) | copy-start | bytes 122884
  60.9 7.3 %copy-start.4 = (f32[192,256]{1,0:T(8,128)}, f32[192,256]{1,0:T(8,128)S(1)}, u32[]{:S(2)}) copy-start(f32[192,256]{1,0:T(8,128)S(1)} %token_stats.1.stat) | copy-start | bytes 589828
  60.9 7.3 %copy-start.2 = (bf16[5120,64]{0,1:T(8,128)(2,1)S(1)}, bf16[5120,64]{0,1:T(8,128)(2,1)}, u32[]{:S(2)}) copy-start(bf16[5120,64]{0,1:T(8,128)(2,1)} %param.15) | copy-start | bytes 1966084
  71.6 0.7 copy-start.6
  72.3 13.6 %copy-start.22 = (bf16[14,24,384]{2,1,0:T(8,128)(2,1)S(1)}, bf16[14,24,384]{2,1,0:T(8,128)(2,1)}, u32[]{:S(2)}) copy-start(bf16[14,24,384]{2,1,0:T(8,128)(2,1)} %get-tuple-element.61) | copy-start | bytes 774148
  72.3 14.7 %copy-start.21 = (bf16[14,24,384]{2,1,0:T(8,128)(2,1)S(1)}, bf16[14,24,384]{2,1,0:T(8,128)(2,1)}, u32[]{:S(2)}) copy-start(bf16[14,24,384]{2,1,0:T(8,128)(2,1)} %get-tuple-element.62) | copy-start | bytes 774148
  72.3 17.1 %copy-start.20 = (bf16[14,24,384]{2,1,0:T(8,128)(2,1)S(1)}, bf16[14,24,384]{2,1,0:T(8,128)(2,1)}, u32[]{:S(2)}) copy-start(bf16[14,24,384]{2,1,0:T(8,128)(2,1)} %get-tuple-element.63) | copy-start | bytes 774148
  72.3 2.2 %collective-permute-start.10 = (bf16[64,24,128]{2,1,0:T(8,128)(2,1)S(1)}, bf16[64,24,128]{2,1,0:T(8,128)(2,1)S(1)}, u32[]{:S(2)}, u32[]{:S(2)}) collective-permute-start(bf16[64,24,128]{2,1,0:T(8,128)(2,1)S(1)} %get-tuple-element.59), channel_id=1, source_target_pairs={{0,32},{1,33},{2,34},{3,35},{4,36},{5,37},{6,38},{7,39},{8,40},{9,... | collective-permute-start | bytes 1179656 | tf_op jit(solution)/shard_map/ppermute | solution.py:613
  75.3 21.5 %all-to-all-start.1 = ((bf16[64,24,128]{2,1,0:T(8,128)(2,1)}), bf16[64,24,128]{2,1,0:T(8,128)(2,1)S(1)}, u32[]{:S(2)}, u32[]{:S(2)}) async-start(bf16[64,24,128]{2,1,0:T(8,128)(2,1)} %add_convert_fusion), calls=%async_computation.1 | async-start | bytes 786432 | tf_op jit(solution)/shard_map/all_to_all | solution.py:615
  85.9 16.8 %collective-permute-start.11 = (bf16[14,24,384]{2,1,0:T(8,128)(2,1)S(1)}, bf16[14,24,384]{2,1,0:T(8,128)(2,1)S(1)}, u32[]{:S(2)}, u32[]{:S(2)}) collective-permute-start(bf16[14,24,384]{2,1,0:T(8,128)(2,1)S(1)} %copy-done.22), channel_id=1, source_target_pairs={{0,4},{1,5},{2,6},{3,7},{4,8},{5,9},{6,10},{7,11},{8,12},{9,13},{1... | collective-permute-start | bytes 774152 | tf_op jit(solution)/shard_map/ppermute | solution.py:616
  87.0 15.7 %collective-permute-start.12 = (bf16[14,24,384]{2,1,0:T(8,128)(2,1)S(1)}, bf16[14,24,384]{2,1,0:T(8,128)(2,1)S(1)}, u32[]{:S(2)}, u32[]{:S(2)}) collective-permute-start(bf16[14,24,384]{2,1,0:T(8,128)(2,1)S(1)} %copy-done.21), channel_id=1, source_target_pairs={{0,8},{1,9},{2,10},{3,11},{4,12},{5,13},{6,14},{7,15},{8,0},{9,1},... | collective-permute-start | bytes 774152 | tf_op jit(solution)/shard_map/ppermute | solution.py:616
  89.4 13.3 %collective-permute-start.13 = (bf16[14,24,384]{2,1,0:T(8,128)(2,1)S(1)}, bf16[14,24,384]{2,1,0:T(8,128)(2,1)S(1)}, u32[]{:S(2)}, u32[]{:S(2)}) collective-permute-start(bf16[14,24,384]{2,1,0:T(8,128)(2,1)S(1)} %copy-done.20), channel_id=1, source_target_pairs={{0,12},{1,13},{2,14},{3,15},{4,0},{5,1},{6,2},{7,3},{8,4},{9,5},{1... | collective-permute-start | bytes 774152 | tf_op jit(solution)/shard_map/ppermute | solution.py:616
  97.7 21.3 %all-to-all-start.2 = ((bf16[64,24,128]{2,1,0:T(8,128)(2,1)}), bf16[64,24,128]{2,1,0:T(8,128)(2,1)S(1)}, u32[]{:S(2)}, u32[]{:S(2)}) async-start(bf16[64,24,128]{2,1,0:T(8,128)(2,1)} %get-tuple-element.66), calls=%async_computation.2 | async-start | bytes 786432 | tf_op jit(solution)/shard_map/all_to_all | solution.py:627
  102.7 0.7 copy-start.13
  102.7 0.8 copy-start.14
  103.5 0.7 copy-start.15
  106.2 12.8 %copy-start.7 = (bf16[14,12,384]{2,1,0:T(8,128)(2,1)S(1)}, bf16[14,12,384]{2,1,0:T(8,128)(2,1)}, u32[]{:S(2)}) copy-start(bf16[14,12,384]{2,1,0:T(8,128)(2,1)} %get-tuple-element.72.same) | copy-start | bytes 387076
  106.2 10.2 %collective-permute-start.14 = (bf16[14,12,384]{2,1,0:T(8,128)(2,1)}, bf16[14,12,384]{2,1,0:T(8,128)(2,1)S(1)}, u32[]{:S(2)}, u32[]{:S(2)}) collective-permute-start(bf16[14,12,384]{2,1,0:T(8,128)(2,1)} %get-tuple-element.72.same), channel_id=1, source_target_pairs={{0,64},{1,65},{2,66},{3,67},{4,68},{5,69},{6,70},{7,71},{8,72},{9,... | collective-permute-start | bytes 387080 | tf_op jit(solution)/shard_map/ppermute | solution.py:624
  108.9 10.1 %collective-permute-start.15 = (bf16[14,12,384]{2,1,0:T(8,128)(2,1)}, bf16[14,12,384]{2,1,0:T(8,128)(2,1)S(1)}, u32[]{:S(2)}, u32[]{:S(2)}) collective-permute-start(bf16[14,12,384]{2,1,0:T(8,128)(2,1)} %get-tuple-element.73), channel_id=1, source_target_pairs={{0,16},{1,17},{2,18},{3,19},{4,20},{5,21},{6,22},{7,23},{8,24},{9,... | collective-permute-start | bytes 387080 | tf_op jit(solution)/shard_map/ppermute | solution.py:625
  109.3 9.7 %collective-permute-start.16 = (bf16[14,12,384]{2,1,0:T(8,128)(2,1)}, bf16[14,12,384]{2,1,0:T(8,128)(2,1)S(1)}, u32[]{:S(2)}, u32[]{:S(2)}) collective-permute-start(bf16[14,12,384]{2,1,0:T(8,128)(2,1)} %get-tuple-element.73), channel_id=1, source_target_pairs={{0,80},{1,81},{2,82},{3,83},{4,84},{5,85},{6,86},{7,87},{8,88},{9,... | collective-permute-start | bytes 387080 | tf_op jit(solution)/shard_map/ppermute | solution.py:626
  119.1 2.4 %collective-permute-start.18 = (f32[14,12,384]{2,1,0:T(8,128)S(1)}, f32[14,12,384]{2,1,0:T(8,128)S(1)}, u32[]{:S(2)}, u32[]{:S(2)}) collective-permute-start(f32[14,12,384]{2,1,0:T(8,128)S(1)} %last_sum.1), channel_id=1, source_target_pairs={{0,32},{1,33},{2,34},{3,35},{4,36},{5,37},{6,38},{7,39},{8,40},{9,... | collective-permute-start | bytes 774152 | tf_op jit(solution)/shard_map/ppermute | solution.py:635
  120.2 2.3 %collective-permute-start.17 = (bf16[64,24,128]{2,1,0:T(8,128)(2,1)S(1)}, bf16[64,24,128]{2,1,0:T(8,128)(2,1)S(1)}, u32[]{:S(2)}, u32[]{:S(2)}) collective-permute-start(bf16[64,24,128]{2,1,0:T(8,128)(2,1)S(1)} %all-to-all-done.2.back), channel_id=1, source_target_pairs={{0,32},{1,33},{2,34},{3,35},{4,36},{5,37},{6,38},{7,39},{8,40},{9,... | collective-permute-start | bytes 1179656 | tf_op jit(solution)/shard_map/ppermute | solution.py:630
  121.5 1.3 %copy-start.3 = (bf16[5120,64]{0,1:T(8,128)(2,1)S(1)}, bf16[5120,64]{0,1:T(8,128)(2,1)}, u32[]{:S(2)}) copy-start(bf16[5120,64]{0,1:T(8,128)(2,1)} %param.15) | copy-start | bytes 1966084
where the time goes:
time: 126 us; the launch traced here: 125 us
  starting transfers between devices  51 us (40%)
  Pallas kernels  43.3 us (34%)
  waiting for transfers between devices  19.9 us (16%)
  local copies, waits for them, and re-layouts  6.05 us (5%)
  other arithmetic  3.84 us (3%)
    pallas_call x1, Pallas kernels, weight_grad(): pl.pallas_call(weight_kernel, grid=(TAPS // 2,), in_specs=[pl.BlockSpec(m...  12.5 us
    pallas_call x1, Pallas kernels, input_grad(): pl.pallas_call(grad_kernel, grid=(3,), in_specs=[whole(2, COLS, SPAN, CH)...  12.4 us
    all_to_all x1, starting transfers between devices, local(): lax.all_to_all(load, BOTH, 0, 0, tiled=True, axis_index_groups=SAME_CORE)  10.5 us
    all_to_all x1, starting transfers between devices, local(): sent = lax.all_to_all(sent, 'tile', 0, 0, tiled=True)  7.86 us
    all_to_all x1, waiting for transfers between devices, local(): lax.all_to_all(load, BOTH, 0, 0, tiled=True, axis_index_groups=SAME_CORE)  6.28 us
    pallas_call x2, Pallas kernels, sum_parts(): pl.pallas_call(sum_kernel, grid=(2,), in_specs=[block(rows)] * 4, out_spe...  5.17 us
    all_to_all x1, starting transfers between devices, local(): lax.all_to_all(back, BOTH, 0, 0, tiled=True, axis_index_groups=SAME_CORE)  4.93 us
    ppermute x3, starting transfers between devices, local(): moved = [lax.ppermute(parts[k], BOTH, along(0, k)) for k in (1, 2, 3)]  4.87 us
  transfers between devices with their start and end apart: 22, of which 9 were waited for; matrix products, arithmetic and copies ran while one was open for 3% of the time, Pallas kernels for 20%

commit v1 on v0

--- a/solution.py
+++ b/solution.py
@@ -531,7 +531,7 @@
         in_specs=[block(rows)] * 4,
         out_specs=[block(rows // count)] * count,
         out_shape=[jax.ShapeDtypeStruct((taps, rows // count, CH), BF16)] * count,
-        compiler_params=pltpu.CompilerParams(vmem_limit_bytes=LARGE),
+        compiler_params=pltpu.CompilerParams(vmem_limit_bytes=LARGE if count == 4 else 16 * 1024 * 1024),
         cost_estimate=pl.CostEstimate(flops=1, bytes_accessed=1, transcendentals=0),
         name="sum_parts",
     )(*terms)

time: 126 us -> 124 us (0.984)
  waiting for transfers between devices: 19.9 us -> 22.2 us
  Pallas kernels: 43.3 us -> 41.5 us
  local copies, waits for them, and re-layouts: 6.05 us -> 4.59 us
    ppermute x1, waiting for transfers between devices: 2.57 us -> 4.87 us  [local(): upper = lax.ppermute(flipped, BOTH, along_y(1))]
    pallas_call x2, Pallas kernels: 5.17 us -> 3.32 us  [sum_parts(): pl.pallas_call(sum_kernel, grid=(2,), in_specs=[block(rows)] * 4, out_spe...]
    unnamed x50 -> x44, local copies, waits for them, and re-layouts: 3.32 us -> 1.86 us
  transfers between devices with their start and end apart: 22 -> 22, of which waited for: 9 -> 9; matrix products, arithmetic and copies ran while one was open for 3% -> 3% of each run, Pallas kernels for 20% -> 19%
where the time goes in v1:
time: 124 us
  starting transfers between devices  50.7 us (41%)
  Pallas kernels  41.5 us (33%)
  waiting for transfers between devices  22.2 us (18%)
  local copies, waits for them, and re-layouts  4.59 us (4%)
  other arithmetic  3.83 us (3%)
    pallas_call x1, Pallas kernels, weight_grad(): pl.pallas_call(weight_kernel, grid=(TAPS // 2,), in_specs=[pl.BlockSpec(m...  12.5 us
    pallas_call x1, Pallas kernels, input_grad(): pl.pallas_call(grad_kernel, grid=(3,), in_specs=[whole(2, COLS, SPAN, CH)...  12.4 us
    all_to_all x1, starting transfers between devices, local(): lax.all_to_all(load, BOTH, 0, 0, tiled=True, axis_index_groups=SAME_CORE)  10.7 us
    all_to_all x1, starting transfers between devices, local(): sent = lax.all_to_all(sent, 'tile', 0, 0, tiled=True)  7.85 us
    all_to_all x1, waiting for transfers between devices, local(): lax.all_to_all(load, BOTH, 0, 0, tiled=True, axis_index_groups=SAME_CORE)  6.28 us
    all_to_all x1, starting transfers between devices, local(): lax.all_to_all(back, BOTH, 0, 0, tiled=True, axis_index_groups=SAME_CORE)  4.93 us
    ppermute x3, starting transfers between devices, local(): moved = [lax.ppermute(parts[k], BOTH, along(0, k)) for k in (1, 2, 3)]  4.88 us
    ppermute x1, waiting for transfers between devices, local(): upper = lax.ppermute(flipped, BOTH, along_y(1))  4.87 us
  transfers between devices with their start and end apart: 22, of which 9 were waited for; matrix products, arithmetic and copies ran while one was open for 3% of the time, Pallas kernels for 19%

profile of v1, /device:TPU:1, one launch (start us, length us, event | category | flops | bytes accessed | tf_op | source)
XLA Modules:
  0.0 123.9 jit_solution(15135542516913871165)
XLA Ops:
  0.6 0.0 copy-start
  0.6 2.3 %fusion.27 = (bf16[2,16,1,12,384]{4,2,3,1,0:T(2,128)(2,1)S(1)}, bf16[2,16,1,12,384]{4,2,3,1,0:T(2,128)(2,1)S(1)}) fusion(bf16[2,16,2,12,384]{4,2,3,1,0:T(2,128)(2,1)} %param.9), kind=kLoop, calls=%fused_computation.60 | loop fusion | bytes 1179648 | tf_op jit(solution)/shard_map/slice | solution.py:574
  3.0 0.0 copy-start.21
  3.0 4.5 %collective-permute-start = (bf16[12,32,384]{2,1,0:T(8,128)(2,1)S(1)}, bf16[12,32,384]{2,1,0:T(8,128)(2,1)S(1)}, u32[]{:S(2)}, u32[]{:S(2)}) collective-permute-start(bf16[12,32,384]{2,1,0:T(8,128)(2,1)S(1)} %bitcast.35), channel_id=1, source_target_pairs={{0,1},{1,2},{2,3},{3,4},{4,5},{5,6},{6,7},{7,8},{8,9},{9,10},{10,1... | collective-permute-start | bytes 884744 | tf_op jit(solution)/shard_map/ppermute | solution.py:577
  7.6 1.3 %collective-permute-start.1 = (bf16[12,32,384]{2,1,0:T(8,128)(2,1)S(1)}, bf16[12,32,384]{2,1,0:T(8,128)(2,1)}, u32[]{:S(2)}, u32[]{:S(2)}) collective-permute-start(bf16[12,32,384]{2,1,0:T(8,128)(2,1)S(1)} %bitcast.34), channel_id=1, source_target_pairs={{1,0},{2,1},{3,2},{4,3},{5,4},{6,5},{7,6},{8,7},{9,8},{10,9},{11,1... | collective-permute-start | bytes 884744 | tf_op jit(solution)/shard_map/ppermute | solution.py:578
  8.9 0.1 fusion.5
  9.0 0.0 copy-start.10
  9.1 0.6 multiply_bitcast_fusion
  9.7 0.1 copy.22
  9.7 0.0 copy-start.11
  9.8 1.0 collective-permute-start.2
  10.8 0.1 copy.27
  10.9 0.4 fusion.3.acts
  11.3 0.4 collective-permute-start.6
  11.7 0.1 reshape.136
  11.7 0.1 broadcast_in_dim.2.keep
  11.8 0.3 collective-permute-start.5
  12.1 1.1 collective-permute-done.low
  13.2 1.5 %collective-permute-start.3 = (bf16[12,32,384]{2,1,0:T(8,128)(2,1)S(1)}, bf16[12,32,384]{2,1,0:T(8,128)(2,1)}, u32[]{:S(2)}, u32[]{:S(2)}) collective-permute-start(bf16[12,32,384]{2,1,0:T(8,128)(2,1)S(1)} %collective-permute-done.low), channel_id=1, source_target_pairs={{0,32},{1,33},{2,34},{3,35},{4,36},{5,37},{6,38},{7,39},{8,40},{9,... | collective-permute-start | bytes 884744 | tf_op jit(solution)/shard_map/ppermute | solution.py:591
  14.7 2.8 %collective-permute-done.1.high = bf16[12,32,384]{2,1,0:T(8,128)(2,1)} collective-permute-done((bf16[12,32,384]{2,1,0:T(8,128)(2,1)S(1)}, bf16[12,32,384]{2,1,0:T(8,128)(2,1)}, u32[]{:S(2)}, u32[]{:S(2)}) %collective-permute-start.1) | collective-permute-done | bytes 294944 | tf_op jit(solution)/shard_map/ppermute | solution.py:578
  17.5 1.7 %collective-permute-start.4 = (bf16[12,32,384]{2,1,0:T(8,128)(2,1)}, bf16[12,32,384]{2,1,0:T(8,128)(2,1)S(1)}, u32[]{:S(2)}, u32[]{:S(2)}) collective-permute-start(bf16[12,32,384]{2,1,0:T(8,128)(2,1)} %collective-permute-done.1.high), channel_id=1, source_target_pairs={{0,32},{1,33},{2,34},{3,35},{4,36},{5,37},{6,38},{7,39},{8,40},{9,... | collective-permute-start | bytes 884744 | tf_op jit(solution)/shard_map/ppermute | solution.py:592
  19.2 0.8 fusion.4.order
  20.1 0.5 collective-permute-done.4.high2
  20.6 0.0 copy-done.20
  20.7 0.2 copy-done.14
  20.9 0.5 copy-done.16
  21.3 12.5 %weight_grad.1 = (bf16[14,96,384]{2,1,0:T(8,128)(2,1)}, bf16[14,96,384]{2,1,0:T(8,128)(2,1)}, bf16[14,96,384]{2,1,0:T(8,128)(2,1)}, bf16[14,96,384]{2,1,0:T(8,128)(2,1)}) custom-call(s32[1]{0:T(128)} %bitcast.core, bf16[2,12,32,384]{3,2,1,0:T(8,128)(2,1)} %bitcast.32, bf16[12,32,384]{2,1,0:T(8,128)(2,1)} %copy-done.15, ...), custom_call_target="tpu_custom_call" | custom-call | flops 6341787648 | bytes 12000000 | tf_op jit(solution)/shard_map/weight_grad/pallas_call | solution.py:245
  33.8 1.3 %collective-permute-start.7 = (bf16[14,96,384]{2,1,0:T(8,128)(2,1)}, bf16[14,96,384]{2,1,0:T(8,128)(2,1)}, u32[]{:S(2)}, u32[]{:S(2)}) collective-permute-start(bf16[14,96,384]{2,1,0:T(8,128)(2,1)} %get-tuple-element.43), channel_id=1, source_target_pairs={{0,1},{1,2},{2,3},{3,0},{4,5},{5,6},{6,7},{7,4},{8,9},{9,10},{10,1... | collective-permute-start | bytes 3096584 | tf_op jit(solution)/shard_map/ppermute | solution.py:602
  35.1 2.5 %collective-permute-start.8 = (bf16[14,96,384]{2,1,0:T(8,128)(2,1)}, bf16[14,96,384]{2,1,0:T(8,128)(2,1)}, u32[]{:S(2)}, u32[]{:S(2)}) collective-permute-start(bf16[14,96,384]{2,1,0:T(8,128)(2,1)} %get-tuple-element.44), channel_id=1, source_target_pairs={{0,2},{1,3},{2,0},{3,1},{4,6},{5,7},{6,4},{7,5},{8,10},{9,11},{10,... | collective-permute-start | bytes 3096584 | tf_op jit(solution)/shard_map/ppermute | solution.py:602
  37.6 1.2 collective-permute-start.9
  38.7 12.4 %input_grad.1 = f32[32,8,128]{2,1,0:T(8,128)} custom-call(bf16[2,12,32,384]{3,2,1,0:T(8,128)(2,1)} %bitcast.33, bf16[12,32,384]{2,1,0:T(8,128)(2,1)} %copy-done.15, bf16[12,32,384]{2,1,0:T(8,128)(2,1)} %collective-permute-done.1.high, bf16[32,384]{1,0:T(8,128)(2,1)} %copy-done.13, bf16[2,12,32,384]{3,2,1,0:T(8,128)(2,1)} %bitcast.28, ...), custom_call_target="tpu_custom_call" | custom-call | flops 6115295232 | bytes 12000000 | tf_op jit(solution)/shard_map/input_grad/pallas_call | solution.py:167
  51.1 7.8 %all-to-all-start = ((f32[32,8,128]{2,1,0:T(8,128)}), f32[32,8,128]{2,1,0:T(8,128)S(1)}, u32[]{:S(2)}, u32[]{:S(2)}) async-start(f32[32,8,128]{2,1,0:T(8,128)} %input_grad.1), calls=%async_computation | async-start | bytes 262144 | tf_op jit(solution)/shard_map/all_to_all | solution.py:608
  59.0 0.0 copy-start.5
  59.1 1.8 %token_stats.1.stat = f32[192,256]{1,0:T(8,128)S(1)} custom-call(bf16[192,5120]{1,0:T(8,128)(2,1)S(1)} %copy-done.1), custom_call_target="tpu_custom_call" | custom-call | flops 1 | bytes 1 | tf_op jit(solution)/shard_map/token_stats/pallas_call | solution.py:283
  60.9 0.0 copy-start.2
  60.9 0.3 collective-permute-done.8.third
  61.2 3.1 %sum_parts.2 = (bf16[14,24,384]{2,1,0:T(8,128)(2,1)}, bf16[14,24,384]{2,1,0:T(8,128)(2,1)}, bf16[14,24,384]{2,1,0:T(8,128)(2,1)}, bf16[14,24,384]{2,1,0:T(8,128)(2,1)}) custom-call(bf16[14,96,384]{2,1,0:T(8,128)(2,1)} %get-tuple-element.42.first, bf16[14,96,384]{2,1,0:T(8,128)(2,1)} %collective-permute-done.7.second, ...), custom_call_target="tpu_custom_call" | custom-call | flops 1 | bytes 1 | tf_op jit(solution)/shard_map/sum_parts/pallas_call | solution.py:528
  64.4 3.8 %all-to-all-done.sent = f32[32,8,128]{2,1,0:T(8,128)S(1)} async-done(((f32[32,8,128]{2,1,0:T(8,128)}), f32[32,8,128]{2,1,0:T(8,128)S(1)}, u32[]{:S(2)}, u32[]{:S(2)}) %all-to-all-start) | async-done | bytes 131104 | tf_op jit(solution)/shard_map/all_to_all | solution.py:608
  68.2 3.4 %head_sums.1 = (bf16[64,24,128]{2,1,0:T(8,128)(2,1)S(1)}, bf16[64,24,128]{2,1,0:T(8,128)(2,1)S(1)}, f32[192,384]{1,0:T(8,128)S(1)}) custom-call(s32[1]{0:T(128)} %bitcast.core, f32[32,8,128]{2,1,0:T(8,128)S(1)} %all-to-all-done.sent, bf16[192,5120]{1,0:T(8,128)(2,1)S(1)} %copy-done.1, bf16[64,5120]{1,0:T(8,128)(2,1)S(1)} %bitcast.26, ...), custom_call_target="tpu_custom_call" | custom-call | flops 503316480 | bytes 7000000 | tf_op jit(solution)/shard_map/head_sums/pallas_call | solution.py:359
  71.6 0.7 copy-done.6
  72.3 0.9 collective-permute-start.10
  73.1 1.3 %collective-permute-done.10 = bf16[64,24,128]{2,1,0:T(8,128)(2,1)S(1)} collective-permute-done((bf16[64,24,128]{2,1,0:T(8,128)(2,1)S(1)}, bf16[64,24,128]{2,1,0:T(8,128)(2,1)S(1)}, u32[]{:S(2)}, u32[]{:S(2)}) %collective-permute-start.10) | collective-permute-done | bytes 393248 | tf_op jit(solution)/shard_map/ppermute | solution.py:613
  74.5 0.8 add_convert_fusion
  75.3 10.7 %all-to-all-start.1 = ((bf16[64,24,128]{2,1,0:T(8,128)(2,1)}), bf16[64,24,128]{2,1,0:T(8,128)(2,1)S(1)}, u32[]{:S(2)}, u32[]{:S(2)}) async-start(bf16[64,24,128]{2,1,0:T(8,128)(2,1)} %add_convert_fusion), calls=%async_computation.1 | async-start | bytes 786432 | tf_op jit(solution)/shard_map/all_to_all | solution.py:615
  86.0 1.1 collective-permute-start.11
  87.1 2.4 %collective-permute-start.12 = (bf16[14,24,384]{2,1,0:T(8,128)(2,1)S(1)}, bf16[14,24,384]{2,1,0:T(8,128)(2,1)S(1)}, u32[]{:S(2)}, u32[]{:S(2)}) collective-permute-start(bf16[14,24,384]{2,1,0:T(8,128)(2,1)S(1)} %copy-done.18), channel_id=1, source_target_pairs={{0,8},{1,9},{2,10},{3,11},{4,12},{5,13},{6,14},{7,15},{8,0},{9,1},... | collective-permute-start | bytes 774152 | tf_op jit(solution)/shard_map/ppermute | solution.py:616
  89.5 1.2 collective-permute-start.13
  90.7 6.3 %all-to-all-done.1.got = bf16[64,24,128]{2,1,0:T(8,128)(2,1)S(1)} async-done(((bf16[64,24,128]{2,1,0:T(8,128)(2,1)}), bf16[64,24,128]{2,1,0:T(8,128)(2,1)S(1)}, u32[]{:S(2)}, u32[]{:S(2)}) %all-to-all-start.1) | async-done | bytes 393248 | tf_op jit(solution)/shard_map/all_to_all | solution.py:615
  97.0 0.9 combine.1
  97.9 4.9 %all-to-all-start.2 = ((bf16[64,24,128]{2,1,0:T(8,128)(2,1)}), bf16[64,24,128]{2,1,0:T(8,128)(2,1)S(1)}, u32[]{:S(2)}, u32[]{:S(2)}) async-start(bf16[64,24,128]{2,1,0:T(8,128)(2,1)} %get-tuple-element.66), calls=%async_computation.2 | async-start | bytes 786432 | tf_op jit(solution)/shard_map/all_to_all | solution.py:627
  102.8 0.2 sum_parts.3
  103.1 2.7 %collective-permute-start.14 = (bf16[14,12,384]{2,1,0:T(8,128)(2,1)S(1)}, bf16[14,12,384]{2,1,0:T(8,128)(2,1)S(1)}, u32[]{:S(2)}, u32[]{:S(2)}) collective-permute-start(bf16[14,12,384]{2,1,0:T(8,128)(2,1)S(1)} %get-tuple-element.72.same), channel_id=1, source_target_pairs={{0,64},{1,65},{2,66},{3,67},{4,68},{5,69},{6,70},{7,71},{8,72},{9,... | collective-permute-start | bytes 387080 | tf_op jit(solution)/shard_map/ppermute | solution.py:624
  105.7 0.4 collective-permute-start.15
  106.1 2.3 %collective-permute-start.16 = (bf16[14,12,384]{2,1,0:T(8,128)(2,1)S(1)}, bf16[14,12,384]{2,1,0:T(8,128)(2,1)S(1)}, u32[]{:S(2)}, u32[]{:S(2)}) collective-permute-start(bf16[14,12,384]{2,1,0:T(8,128)(2,1)S(1)} %get-tuple-element.73), channel_id=1, source_target_pairs={{0,80},{1,81},{2,82},{3,83},{4,84},{5,85},{6,86},{7,87},{8,88},{9,... | collective-permute-start | bytes 387080 | tf_op jit(solution)/shard_map/ppermute | solution.py:626
  108.4 4.8 %hidden_grads.1 = bf16[192,5120]{1,0:T(8,128)(2,1)} custom-call(f32[192,384]{1,0:T(8,128)} %copy-done.6, bf16[192,5120]{1,0:T(8,128)(2,1)} %states.4, bf16[64,5120]{1,0:T(8,128)(2,1)} %bitcast.25, f32[2,5120]{1,0:T(2,128)} %copy-done.5, f32[192,256]{1,0:T(8,128)} %copy-done.4), custom_call_target="tpu_custom_call" | custom-call | flops 251658240 | bytes 6000000 | tf_op jit(solution)/shard_map/hidden_grads/pallas_call | solution.py:486
  113.3 4.9 %collective-permute-done.15.upper = bf16[14,12,384]{2,1,0:T(8,128)(2,1)S(1)} collective-permute-done((bf16[14,12,384]{2,1,0:T(8,128)(2,1)S(1)}, bf16[14,12,384]{2,1,0:T(8,128)(2,1)S(1)}, u32[]{:S(2)}, u32[]{:S(2)}) %collective-permute-start.15) | collective-permute-done | bytes 129056 | tf_op jit(solution)/shard_map/ppermute | solution.py:625
  118.1 0.1 last_sum.1
  118.2 0.7 collective-permute-start.18
  119.0 0.1 collective-permute-start.17
  119.1 0.1 pad_add_fusion.place_at
  119.1 1.1 collective-permute-done.18
  120.4 0.9 pad_maximum_fusion
  121.3 0.4 copy-done.3
  121.6 2.3 %unpack.1 = (f32[64,5120]{1,0:T(8,128)}, f32[2,2,5120]{2,1,0:T(2,128)}) custom-call(s32[2]{0:T(128)S(1)} %pad_add_fusion.place_at, bf16[64,24,128]{2,1,0:T(8,128)(2,1)S(1)} %all-to-all-done.2.back, bf16[64,24,128]{2,1,0:T(8,128)(2,1)S(1)} %collective-permute-done.17.theirs, f32[8,128]{1,0:T(8,128)S(1)} %get-tuple-element.76.whole, bf16[64,5120]{1,0:T(8,128)(2,1)S(1)} %bitcast.27), custom_call_target="tpu_custom_call" | custom-call | flops 10000000 | bytes 3000000 | tf_op jit(solution)/shard_map/unpack/pallas_call | solution.py:457
  (54 shorter events, 0.3 us)
Async XLA Ops:
  0.6 58.4 %copy-start = (f32[2,2,5120]{2,1,0:T(2,128)S(1)}, f32[2,2,5120]{2,1,0:T(2,128)}, u32[]{:S(2)}) copy-start(f32[2,2,5120]{2,1,0:T(2,128)} %param.14) | copy-start | bytes 245764
  3.0 6.0 %copy-start.21 = (s32[2,16]{1,0:T(2,128)S(1)}, s32[2,16]{1,0:T(2,128)}, u32[]{:S(2)}) copy-start(s32[2,16]{1,0:T(2,128)} %param.10) | copy-start | bytes 388
  3.0 6.1 %copy-start.8 = (bf16[2,16,2,12,384]{4,2,3,1,0:T(2,128)(2,1)S(1)}, bf16[2,16,2,12,384]{4,2,3,1,0:T(2,128)(2,1)}, u32[]{:S(2)}) copy-start(bf16[2,16,2,12,384]{4,2,3,1,0:T(2,128)(2,1)} %param.9) | copy-start | bytes 1769476
  3.0 10.2 %collective-permute-start = (bf16[12,32,384]{2,1,0:T(8,128)(2,1)S(1)}, bf16[12,32,384]{2,1,0:T(8,128)(2,1)S(1)}, u32[]{:S(2)}, u32[]{:S(2)}) collective-permute-start(bf16[12,32,384]{2,1,0:T(8,128)(2,1)S(1)} %bitcast.35), channel_id=1, source_target_pairs={{0,1},{1,2},{2,3},{3,4},{4,5},{5,6},{6,7},{7,8},{8,9},{9,10},{10,1... | collective-permute-start | bytes 884744 | tf_op jit(solution)/shard_map/ppermute | solution.py:577
  7.6 9.9 %collective-permute-start.1 = (bf16[12,32,384]{2,1,0:T(8,128)(2,1)S(1)}, bf16[12,32,384]{2,1,0:T(8,128)(2,1)}, u32[]{:S(2)}, u32[]{:S(2)}) collective-permute-start(bf16[12,32,384]{2,1,0:T(8,128)(2,1)S(1)} %bitcast.34), channel_id=1, source_target_pairs={{1,0},{2,1},{3,2},{4,3},{5,4},{6,5},{7,6},{8,7},{9,8},{10,9},{11,1... | collective-permute-start | bytes 884744 | tf_op jit(solution)/shard_map/ppermute | solution.py:578
  9.0 1.7 %copy-start.10 = (bf16[2,16,2,12,384]{4,2,3,1,0:T(2,128)(2,1)S(1)}, bf16[2,16,2,12,384]{4,2,3,1,0:T(2,128)(2,1)}, u32[]{:S(2)}) copy-start(bf16[2,16,2,12,384]{4,2,3,1,0:T(2,128)(2,1)} %param.8) | copy-start | bytes 1769476
  9.7 1.5 %copy-start.11 = (bf16[2,12,2,16,384]{4,3,2,1,0:T(8,128)(2,1)}, bf16[2,12,2,16,384]{4,3,2,1,0:T(8,128)(2,1)S(1)}, u32[]{:S(2)}) copy-start(bf16[2,12,2,16,384]{4,3,2,1,0:T(8,128)(2,1)S(1)} %copy.22) | copy-start | bytes 1769476
  9.8 10.3 %collective-permute-start.2 = (bf16[2,12,32,384]{3,2,1,0:T(8,128)(2,1)S(1)}, bf16[2,12,32,384]{3,2,1,0:T(8,128)(2,1)S(1)}, u32[]{:S(2)}, u32[]{:S(2)}) collective-permute-start(bf16[2,12,32,384]{3,2,1,0:T(8,128)(2,1)S(1)} %bitcast.31), channel_id=1, source_target_pairs={{0,32},{1,33},{2,34},{3,35},{4,36},{5,37},{6,38},{7,39},{8,40},{9,... | collective-permute-start | bytes 1769480 | tf_op jit(solution)/shard_map/ppermute | solution.py:587
  10.9 22.9 %copy-start.9 = (bf16[2,12,2,16,384]{4,3,2,1,0:T(8,128)(2,1)}, bf16[2,12,2,16,384]{4,3,2,1,0:T(8,128)(2,1)S(1)}, u32[]{:S(2)}) copy-start(bf16[2,12,2,16,384]{4,3,2,1,0:T(8,128)(2,1)S(1)} %copy.27) | copy-start | bytes 1769476
  11.3 9.3 %copy-start.12 = (bf16[2,12,32,384]{3,2,1,0:T(8,128)(2,1)}, bf16[2,12,32,384]{3,2,1,0:T(8,128)(2,1)S(1)}, u32[]{:S(2)}) copy-start(bf16[2,12,32,384]{3,2,1,0:T(8,128)(2,1)S(1)} %fusion.3.acts) | copy-start | bytes 1769476
  11.3 9.3 %collective-permute-start.6 = (bf16[2,12,32,384]{3,2,1,0:T(8,128)(2,1)S(1)}, bf16[2,12,32,384]{3,2,1,0:T(8,128)(2,1)}, u32[]{:S(2)}, u32[]{:S(2)}) collective-permute-start(bf16[2,12,32,384]{3,2,1,0:T(8,128)(2,1)S(1)} %fusion.3.acts), channel_id=1, source_target_pairs={{0,32},{1,33},{2,34},{3,35},{4,36},{5,37},{6,38},{7,39},{8,40},{9,... | collective-permute-start | bytes 1769480 | tf_op jit(solution)/shard_map/ppermute | solution.py:589
  11.8 8.8 %copy-start.13 = (bf16[32,384]{1,0:T(8,128)(2,1)}, bf16[32,384]{1,0:T(8,128)(2,1)S(1)}, u32[]{:S(2)}) copy-start(bf16[32,384]{1,0:T(8,128)(2,1)S(1)} %broadcast_in_dim.2.keep) | copy-start | bytes 73732
  11.8 8.2 %collective-permute-start.5 = (bf16[32,384]{1,0:T(8,128)(2,1)S(1)}, bf16[32,384]{1,0:T(8,128)(2,1)S(1)}, u32[]{:S(2)}, u32[]{:S(2)}) collective-permute-start(bf16[32,384]{1,0:T(8,128)(2,1)S(1)} %broadcast_in_dim.2.keep), channel_id=1, source_target_pairs={{0,32},{1,33},{2,34},{3,35},{4,36},{5,37},{6,38},{7,39},{8,40},{9,... | collective-permute-start | bytes 73736 | tf_op jit(solution)/shard_map/ppermute | solution.py:590
  13.2 7.4 %copy-start.15 = (bf16[12,32,384]{2,1,0:T(8,128)(2,1)}, bf16[12,32,384]{2,1,0:T(8,128)(2,1)S(1)}, u32[]{:S(2)}) copy-start(bf16[12,32,384]{2,1,0:T(8,128)(2,1)S(1)} %collective-permute-done.low) | copy-start | bytes 884740
  13.2 6.9 %collective-permute-start.3 = (bf16[12,32,384]{2,1,0:T(8,128)(2,1)S(1)}, bf16[12,32,384]{2,1,0:T(8,128)(2,1)}, u32[]{:S(2)}, u32[]{:S(2)}) collective-permute-start(bf16[12,32,384]{2,1,0:T(8,128)(2,1)S(1)} %collective-permute-done.low), channel_id=1, source_target_pairs={{0,32},{1,33},{2,34},{3,35},{4,36},{5,37},{6,38},{7,39},{8,40},{9,... | collective-permute-start | bytes 884744 | tf_op jit(solution)/shard_map/ppermute | solution.py:591
  17.5 3.1 %collective-permute-start.4 = (bf16[12,32,384]{2,1,0:T(8,128)(2,1)}, bf16[12,32,384]{2,1,0:T(8,128)(2,1)S(1)}, u32[]{:S(2)}, u32[]{:S(2)}) collective-permute-start(bf16[12,32,384]{2,1,0:T(8,128)(2,1)} %collective-permute-done.1.high), channel_id=1, source_target_pairs={{0,32},{1,33},{2,34},{3,35},{4,36},{5,37},{6,38},{7,39},{8,40},{9,... | collective-permute-start | bytes 884744 | tf_op jit(solution)/shard_map/ppermute | solution.py:592
  20.1 0.6 copy-start.20
  20.1 0.8 copy-start.14
  20.6 0.7 copy-start.16
  33.8 27.1 %collective-permute-start.7 = (bf16[14,96,384]{2,1,0:T(8,128)(2,1)}, bf16[14,96,384]{2,1,0:T(8,128)(2,1)}, u32[]{:S(2)}, u32[]{:S(2)}) collective-permute-start(bf16[14,96,384]{2,1,0:T(8,128)(2,1)} %get-tuple-element.43), channel_id=1, source_target_pairs={{0,1},{1,2},{2,3},{3,0},{4,5},{5,6},{6,7},{7,4},{8,9},{9,10},{10,1... | collective-permute-start | bytes 3096584 | tf_op jit(solution)/shard_map/ppermute | solution.py:602
  35.1 26.1 %collective-permute-start.8 = (bf16[14,96,384]{2,1,0:T(8,128)(2,1)}, bf16[14,96,384]{2,1,0:T(8,128)(2,1)}, u32[]{:S(2)}, u32[]{:S(2)}) collective-permute-start(bf16[14,96,384]{2,1,0:T(8,128)(2,1)} %get-tuple-element.44), channel_id=1, source_target_pairs={{0,2},{1,3},{2,0},{3,1},{4,6},{5,7},{6,4},{7,5},{8,10},{9,11},{10,... | collective-permute-start | bytes 3096584 | tf_op jit(solution)/shard_map/ppermute | solution.py:602
  37.6 23.7 %collective-permute-start.9 = (bf16[14,96,384]{2,1,0:T(8,128)(2,1)}, bf16[14,96,384]{2,1,0:T(8,128)(2,1)}, u32[]{:S(2)}, u32[]{:S(2)}) collective-permute-start(bf16[14,96,384]{2,1,0:T(8,128)(2,1)} %get-tuple-element.45), channel_id=1, source_target_pairs={{0,3},{1,0},{2,1},{3,2},{4,7},{5,4},{6,5},{7,6},{8,11},{9,8},{10,9... | collective-permute-start | bytes 3096584 | tf_op jit(solution)/shard_map/ppermute | solution.py:602
  38.7 20.3 %copy-start.1 = (bf16[192,5120]{1,0:T(8,128)(2,1)S(1)}, bf16[192,5120]{1,0:T(8,128)(2,1)}, u32[]{:S(2)}) copy-start(bf16[192,5120]{1,0:T(8,128)(2,1)} %states.4) | copy-start | bytes 5898244
  51.1 17.0 %all-to-all-start = ((f32[32,8,128]{2,1,0:T(8,128)}), f32[32,8,128]{2,1,0:T(8,128)S(1)}, u32[]{:S(2)}, u32[]{:S(2)}) async-start(f32[32,8,128]{2,1,0:T(8,128)} %input_grad.1), calls=%async_computation | async-start | bytes 262144 | tf_op jit(solution)/shard_map/all_to_all | solution.py:608
  59.0 9.1 %copy-start.5 = (f32[2,5120]{1,0:T(2,128)}, f32[2,5120]{1,0:T(2,128)S(1)}, u32[]{:S(2)}) copy-start(f32[2,5120]{1,0:T(2,128)S(1)} %dynamic-slice_bitcast_fusion.mods) | copy-start | bytes 122884
  60.9 7.3 %copy-start.4 = (f32[192,256]{1,0:T(8,128)}, f32[192,256]{1,0:T(8,128)S(1)}, u32[]{:S(2)}) copy-start(f32[192,256]{1,0:T(8,128)S(1)} %token_stats.1.stat) | copy-start | bytes 589828
  60.9 7.3 %copy-start.2 = (bf16[5120,64]{0,1:T(8,128)(2,1)S(1)}, bf16[5120,64]{0,1:T(8,128)(2,1)}, u32[]{:S(2)}) copy-start(bf16[5120,64]{0,1:T(8,128)(2,1)} %param.15) | copy-start | bytes 1966084
  71.6 0.7 copy-start.6
  72.3 13.8 %copy-start.19 = (bf16[14,24,384]{2,1,0:T(8,128)(2,1)S(1)}, bf16[14,24,384]{2,1,0:T(8,128)(2,1)}, u32[]{:S(2)}) copy-start(bf16[14,24,384]{2,1,0:T(8,128)(2,1)} %get-tuple-element.61) | copy-start | bytes 774148
  72.3 14.8 %copy-start.18 = (bf16[14,24,384]{2,1,0:T(8,128)(2,1)S(1)}, bf16[14,24,384]{2,1,0:T(8,128)(2,1)}, u32[]{:S(2)}) copy-start(bf16[14,24,384]{2,1,0:T(8,128)(2,1)} %get-tuple-element.62) | copy-start | bytes 774148
  72.3 17.2 %copy-start.17 = (bf16[14,24,384]{2,1,0:T(8,128)(2,1)S(1)}, bf16[14,24,384]{2,1,0:T(8,128)(2,1)}, u32[]{:S(2)}) copy-start(bf16[14,24,384]{2,1,0:T(8,128)(2,1)} %get-tuple-element.63) | copy-start | bytes 774148
  72.3 2.2 %collective-permute-start.10 = (bf16[64,24,128]{2,1,0:T(8,128)(2,1)S(1)}, bf16[64,24,128]{2,1,0:T(8,128)(2,1)S(1)}, u32[]{:S(2)}, u32[]{:S(2)}) collective-permute-start(bf16[64,24,128]{2,1,0:T(8,128)(2,1)S(1)} %get-tuple-element.59), channel_id=1, source_target_pairs={{0,32},{1,33},{2,34},{3,35},{4,36},{5,37},{6,38},{7,39},{8,40},{9,... | collective-permute-start | bytes 1179656 | tf_op jit(solution)/shard_map/ppermute | solution.py:613
  75.3 27.5 %copy-start.7 = (bf16[14,24,384]{2,1,0:T(8,128)(2,1)S(1)}, bf16[14,24,384]{2,1,0:T(8,128)(2,1)}, u32[]{:S(2)}) copy-start(bf16[14,24,384]{2,1,0:T(8,128)(2,1)} %get-tuple-element.64.first) | copy-start | bytes 774148
  75.3 21.6 %all-to-all-start.1 = ((bf16[64,24,128]{2,1,0:T(8,128)(2,1)}), bf16[64,24,128]{2,1,0:T(8,128)(2,1)S(1)}, u32[]{:S(2)}, u32[]{:S(2)}) async-start(bf16[64,24,128]{2,1,0:T(8,128)(2,1)} %add_convert_fusion), calls=%async_computation.1 | async-start | bytes 786432 | tf_op jit(solution)/shard_map/all_to_all | solution.py:615
  86.0 16.8 %collective-permute-start.11 = (bf16[14,24,384]{2,1,0:T(8,128)(2,1)S(1)}, bf16[14,24,384]{2,1,0:T(8,128)(2,1)S(1)}, u32[]{:S(2)}, u32[]{:S(2)}) collective-permute-start(bf16[14,24,384]{2,1,0:T(8,128)(2,1)S(1)} %copy-done.19), channel_id=1, source_target_pairs={{0,4},{1,5},{2,6},{3,7},{4,8},{5,9},{6,10},{7,11},{8,12},{9,13},{1... | collective-permute-start | bytes 774152 | tf_op jit(solution)/shard_map/ppermute | solution.py:616
  87.1 15.7 %collective-permute-start.12 = (bf16[14,24,384]{2,1,0:T(8,128)(2,1)S(1)}, bf16[14,24,384]{2,1,0:T(8,128)(2,1)S(1)}, u32[]{:S(2)}, u32[]{:S(2)}) collective-permute-start(bf16[14,24,384]{2,1,0:T(8,128)(2,1)S(1)} %copy-done.18), channel_id=1, source_target_pairs={{0,8},{1,9},{2,10},{3,11},{4,12},{5,13},{6,14},{7,15},{8,0},{9,1},... | collective-permute-start | bytes 774152 | tf_op jit(solution)/shard_map/ppermute | solution.py:616
  89.5 13.3 %collective-permute-start.13 = (bf16[14,24,384]{2,1,0:T(8,128)(2,1)S(1)}, bf16[14,24,384]{2,1,0:T(8,128)(2,1)S(1)}, u32[]{:S(2)}, u32[]{:S(2)}) collective-permute-start(bf16[14,24,384]{2,1,0:T(8,128)(2,1)S(1)} %copy-done.17), channel_id=1, source_target_pairs={{0,12},{1,13},{2,14},{3,15},{4,0},{5,1},{6,2},{7,3},{8,4},{9,5},{1... | collective-permute-start | bytes 774152 | tf_op jit(solution)/shard_map/ppermute | solution.py:616
  97.9 20.4 %all-to-all-start.2 = ((bf16[64,24,128]{2,1,0:T(8,128)(2,1)}), bf16[64,24,128]{2,1,0:T(8,128)(2,1)S(1)}, u32[]{:S(2)}, u32[]{:S(2)}) async-start(bf16[64,24,128]{2,1,0:T(8,128)(2,1)} %get-tuple-element.66), calls=%async_computation.2 | async-start | bytes 786432 | tf_op jit(solution)/shard_map/all_to_all | solution.py:627
  103.1 10.2 %collective-permute-start.14 = (bf16[14,12,384]{2,1,0:T(8,128)(2,1)S(1)}, bf16[14,12,384]{2,1,0:T(8,128)(2,1)S(1)}, u32[]{:S(2)}, u32[]{:S(2)}) collective-permute-start(bf16[14,12,384]{2,1,0:T(8,128)(2,1)S(1)} %get-tuple-element.72.same), channel_id=1, source_target_pairs={{0,64},{1,65},{2,66},{3,67},{4,68},{5,69},{6,70},{7,71},{8,72},{9,... | collective-permute-start | bytes 387080 | tf_op jit(solution)/shard_map/ppermute | solution.py:624
  105.7 12.4 %collective-permute-start.15 = (bf16[14,12,384]{2,1,0:T(8,128)(2,1)S(1)}, bf16[14,12,384]{2,1,0:T(8,128)(2,1)S(1)}, u32[]{:S(2)}, u32[]{:S(2)}) collective-permute-start(bf16[14,12,384]{2,1,0:T(8,128)(2,1)S(1)} %get-tuple-element.73), channel_id=1, source_target_pairs={{0,16},{1,17},{2,18},{3,19},{4,20},{5,21},{6,22},{7,23},{8,24},{9,... | collective-permute-start | bytes 387080 | tf_op jit(solution)/shard_map/ppermute | solution.py:625
  106.1 12.0 %collective-permute-start.16 = (bf16[14,12,384]{2,1,0:T(8,128)(2,1)S(1)}, bf16[14,12,384]{2,1,0:T(8,128)(2,1)S(1)}, u32[]{:S(2)}, u32[]{:S(2)}) collective-permute-start(bf16[14,12,384]{2,1,0:T(8,128)(2,1)S(1)} %get-tuple-element.73), channel_id=1, source_target_pairs={{0,80},{1,81},{2,82},{3,83},{4,84},{5,85},{6,86},{7,87},{8,88},{9,... | collective-permute-start | bytes 387080 | tf_op jit(solution)/shard_map/ppermute | solution.py:626
  118.2 2.0 %collective-permute-start.18 = (f32[14,12,384]{2,1,0:T(8,128)S(1)}, f32[14,12,384]{2,1,0:T(8,128)S(1)}, u32[]{:S(2)}, u32[]{:S(2)}) collective-permute-start(f32[14,12,384]{2,1,0:T(8,128)S(1)} %last_sum.1), channel_id=1, source_target_pairs={{0,32},{1,33},{2,34},{3,35},{4,36},{5,37},{6,38},{7,39},{8,40},{9,... | collective-permute-start | bytes 774152 | tf_op jit(solution)/shard_map/ppermute | solution.py:635
  119.0 2.3 %collective-permute-start.17 = (bf16[64,24,128]{2,1,0:T(8,128)(2,1)S(1)}, bf16[64,24,128]{2,1,0:T(8,128)(2,1)S(1)}, u32[]{:S(2)}, u32[]{:S(2)}) collective-permute-start(bf16[64,24,128]{2,1,0:T(8,128)(2,1)S(1)} %all-to-all-done.2.back), channel_id=1, source_target_pairs={{0,32},{1,33},{2,34},{3,35},{4,36},{5,37},{6,38},{7,39},{8,40},{9,... | collective-permute-start | bytes 1179656 | tf_op jit(solution)/shard_map/ppermute | solution.py:630
  120.3 1.3 %copy-start.3 = (bf16[5120,64]{0,1:T(8,128)(2,1)S(1)}, bf16[5120,64]{0,1:T(8,128)(2,1)}, u32[]{:S(2)}) copy-start(bf16[5120,64]{0,1:T(8,128)(2,1)} %param.15) | copy-start | bytes 1966084
